TPU v7x, 512 devices: a whole 4x4x16 slice. The times are simulated.
512 devices in a mesh: gx: 16 (over z), gy: 8 (over x, core), gz: 4 (over y).
Axes of the slice: x: 4, y: 4, z: 16, core: 2. Of those that a mesh axis runs over, the one named last changes fastest.
Arguments:
- fields: float32 [2, 8, 1024, 1024], P(None, 'gz', 'gx', 'gy'), may hold values from -6 to 6
- conductivity: float32 [2, 8, 1024, 1024], P(None, 'gz', 'gx', 'gy'), may hold values from 0.5 to 2
- source: float32 [2, 8, 1024, 1024], P(None, 'gz', 'gx', 'gy'), may hold values from -3072 to 3072
Outputs:
- advanced: float32 [2, 8, 1024, 1024], P(None, 'gz', 'gx', 'gy')
All inputs are finite; a program needn't handle non-finite values.
Results may differ from a plain program's by a relative error of at most 0.008.
Values sent between devices are 32-bit elements; how exact they have to be, the bound alone decides.
No kernel may reach another device: no remote copies, remote signals or barrier semaphores. Data moves between devices by JAX's collectives and lax.ppermute only.
A program may use at most 64 MiB of HBM per device.

v0:
```python
import jax
import jax.numpy as jnp
from jax import lax
from jax.sharding import PartitionSpec as P

WEIGHT_IMPLICIT = 0.5


def extended(x, sides, width):
    for axis, dim in sides:
        peers, length = (lax.axis_size(axis), x.shape[dim])
        up = [(i, (i + 1) % peers) for i in range(peers - 1)]
        down = [(j, i) for i, j in up]
        last = lax.slice_in_dim(x, length - width, length, axis=dim)
        leading = lax.slice_in_dim(x, 0, width, axis=dim)
        before = lax.ppermute(last, axis, up)
        after = lax.ppermute(leading, axis, down)
        x = jnp.concatenate([before, x, after], axis=dim)
    return x


def inner_view(padded, axis_dim):
    selection = [slice(None)]
    for spatial in (1, 2, 3):
        selection.append(slice(None) if spatial == axis_dim else slice(1, -1))
    return padded[tuple(selection)]


def face_values(kappa_view, axis_dim):
    extent = kappa_view.shape[axis_dim]
    return 0.5 * (
        lax.slice_in_dim(kappa_view, 1, extent, axis=axis_dim)
        + lax.slice_in_dim(kappa_view, 0, extent - 1, axis=axis_dim)
    )


def flux_term(field_now, field_view, face_kappa, axis_dim):
    extent = field_now.shape[axis_dim]
    next_cell = lax.slice_in_dim(field_view, 2, extent + 2, axis=axis_dim)
    prev_cell = lax.slice_in_dim(field_view, 0, extent, axis=axis_dim)
    upper_face = lax.slice_in_dim(face_kappa, 1, extent + 1, axis=axis_dim)
    lower_face = lax.slice_in_dim(face_kappa, 0, extent, axis=axis_dim)
    return upper_face * (next_cell - field_now) - lower_face * (field_now - prev_cell)


def shifted(values, stride, axis_dim, fill_value, from_below):
    extent = values.shape[axis_dim]
    pad_shape = list(values.shape)
    pad_shape[axis_dim] = stride
    padding = jnp.full(pad_shape, fill_value, values.dtype)
    if from_below:
        return jnp.concatenate(
            [padding, lax.slice_in_dim(values, 0, extent - stride, axis=axis_dim)], axis_dim
        )
    return jnp.concatenate(
        [lax.slice_in_dim(values, stride, extent, axis=axis_dim), padding], axis_dim
    )


def cyclic_solve(lower_band, main_band, upper_band, targets, axis_dim):
    extent = main_band.shape[axis_dim]
    stride = 1
    while stride < extent:
        ratio_low = lower_band / shifted(main_band, stride, axis_dim, 1.0, True)
        ratio_high = upper_band / shifted(main_band, stride, axis_dim, 1.0, False)
        main_band = (
            main_band
            - ratio_low * shifted(upper_band, stride, axis_dim, 0.0, True)
            - ratio_high * shifted(lower_band, stride, axis_dim, 0.0, False)
        )
        targets = tuple(
            (
                vector
                - ratio_low * shifted(vector, stride, axis_dim, 0.0, True)
                - ratio_high * shifted(vector, stride, axis_dim, 0.0, False)
                for vector in targets
            )
        )
        lower_band, upper_band = (
            -ratio_low * shifted(lower_band, stride, axis_dim, 0.0, True),
            -ratio_high * shifted(upper_band, stride, axis_dim, 0.0, False),
        )
        stride = stride * 2
    return tuple((vector / main_band for vector in targets))


def local_sweep(target, face_kappa, axis_dim, diffusion):
    extent = target.shape[axis_dim]
    interior = extent - 1
    scale_factor = WEIGHT_IMPLICIT * diffusion
    lower_band = -scale_factor * lax.slice_in_dim(face_kappa, 0, extent, axis=axis_dim)
    upper_band = -scale_factor * lax.slice_in_dim(face_kappa, 1, extent + 1, axis=axis_dim)
    main_band = 1.0 - lower_band - upper_band
    first_row = lax.slice_in_dim(lower_band, 0, 1, axis=axis_dim)
    last_row = lax.slice_in_dim(upper_band, interior - 1, interior, axis=axis_dim)
    zero_shape = list(target.shape)
    zero_shape[axis_dim] = interior - 1
    zero_rows = jnp.zeros(zero_shape, jnp.float32)
    left_unit = jnp.concatenate([-first_row, zero_rows], axis_dim)
    right_unit = jnp.concatenate([zero_rows, -last_row], axis_dim)

    def leading(values):
        return lax.slice_in_dim(values, 0, interior, axis=axis_dim)

    base_part, from_left, from_right = cyclic_solve(
        leading(lower_band),
        leading(main_band),
        leading(upper_band),
        (leading(target), left_unit, right_unit),
        axis_dim,
    )

    def row_at(values, position):
        return lax.index_in_dim(values, position, axis=axis_dim, keepdims=False)

    pieces = jnp.stack(
        [
            row_at(lower_band, interior),
            row_at(main_band, interior),
            row_at(upper_band, interior),
            row_at(target, interior),
            row_at(base_part, interior - 1),
            row_at(from_left, interior - 1),
            row_at(from_right, interior - 1),
            row_at(base_part, 0),
            row_at(from_left, 0),
            row_at(from_right, 0),
        ],
        0,
    )
    return (pieces, (base_part, from_left, from_right))


def reduced_solve(pieces):
    members = [pieces[:, number] for number in range(10)]
    (
        sep_lower,
        sep_main,
        sep_upper,
        sep_right,
        base_last,
        left_last,
        right_last,
        base_first,
        left_first,
        right_first,
    ) = members
    next_base = shifted(base_first, 1, 0, 0.0, False)
    next_left = shifted(left_first, 1, 0, 0.0, False)
    next_right = shifted(right_first, 1, 0, 0.0, False)
    coupling_low = sep_lower * left_last
    diagonal = sep_main + sep_lower * right_last + sep_upper * next_left
    coupling_high = sep_upper * next_right
    target = sep_right - sep_lower * base_last - sep_upper * next_base
    return cyclic_solve(coupling_low, diagonal, coupling_high, (target,), 0)[0]


def own_lines(lines_all, position):
    own_line = lax.dynamic_index_in_dim(lines_all, position, 0, keepdims=False)
    earlier = lax.dynamic_index_in_dim(lines_all, jnp.maximum(position - 1, 0), 0, keepdims=False)
    return (own_line, earlier * (position > 0).astype(jnp.float32))


def finish(solution, previous, local_parts, axis_dim):
    base_part, from_left, from_right = local_parts
    own_edge = jnp.expand_dims(solution, axis_dim)
    interior_cells = (
        base_part + from_left * jnp.expand_dims(previous, axis_dim) + from_right * own_edge
    )
    return jnp.concatenate([interior_cells, own_edge], axis_dim)


def on_device(fields, conductivity, source):
    cells_x = fields.shape[2] * lax.axis_size("gx")
    cells_y = fields.shape[3] * lax.axis_size("gy")
    diffusion = float(4 * fields.shape[2] * fields.shape[2])
    vertical = float((cells_x + cells_y) // 8)
    stacked = jnp.concatenate([fields, conductivity], 0)
    padded = extended(stacked, (("gx", 2), ("gy", 3), ("gz", 1)), 1)
    count_fields = fields.shape[0]
    field_pad = padded[:count_fields]
    kappa_pad = padded[count_fields:]
    faces_by_dim = {}
    increment = source
    for axis_dim, number in ((2, diffusion), (3, diffusion), (1, vertical)):
        face_kappa = face_values(inner_view(kappa_pad, axis_dim), axis_dim)
        faces_by_dim[axis_dim] = face_kappa
        increment = increment + number * flux_term(
            fields, inner_view(field_pad, axis_dim), face_kappa, axis_dim
        )
    pieces, local_parts = local_sweep(increment, faces_by_dim[2], 2, diffusion)
    gathered = lax.all_gather(pieces[None], "gx", axis=0, tiled=True)
    solution, previous = own_lines(reduced_solve(gathered), lax.axis_index("gx"))
    swept_first = finish(solution, previous, local_parts, 2)
    pieces, local_parts = local_sweep(swept_first, faces_by_dim[3], 3, diffusion)
    gathered = lax.all_gather(pieces[None], "gy", axis=0, tiled=True)
    solution, previous = own_lines(reduced_solve(gathered), lax.axis_index("gy"))
    second = finish(solution, previous, local_parts, 3)
    return fields + second


def solution(mesh):
    in_specs = (P(None, "gz", "gx", "gy"), P(None, "gz", "gx", "gy"), P(None, "gz", "gx", "gy"))
    out_specs = P(None, "gz", "gx", "gy")
    return jax.shard_map(
        on_device, mesh=mesh, in_specs=in_specs, out_specs=out_specs, check_vma=False
    )
```

profile of v0, /device:TPU:1, one launch (start us, length us, event | category | flops | bytes accessed | tf_op | source)
XLA Modules:
  0.0 124.8 jit_solution(2804154696957513523)
XLA Ops:
  0.0 1.0 constant_dynamic-update-slice_fusion
  1.2 1.3 %collective-permute-start = (f32[4,2,1,128]{3,1,0,2:T(2,128)S(1)}, f32[4,2,1,128]{3,1,0,2:T(2,128)S(1)}, u32[]{:S(2)}, u32[]{:S(2)}) collective-permute-start(f32[4,2,1,128]{3,1,0,2:T(2,128)S(1)} %get-tuple-element.105), channel_id=1, source_target_pairs={{32,0},{64,32},{96,64},{128,96},{160,128},{192,160},{224,192},{256... | collective-permute-start | bytes 12296 | tf_op jit(solution)/shard_map/ppermute | solution.py:17
  2.5 5.0 %collective-permute-start.1 = (f32[4,2,1,128]{3,1,0,2:T(2,128)S(1)}, f32[4,2,1,128]{3,1,0,2:T(2,128)S(1)}, u32[]{:S(2)}, u32[]{:S(2)}) collective-permute-start(f32[4,2,1,128]{3,1,0,2:T(2,128)S(1)} %get-tuple-element.104), channel_id=1, source_target_pairs={{0,32},{32,64},{64,96},{96,128},{128,160},{160,192},{192,224},{224... | collective-permute-start | bytes 12296 | tf_op jit(solution)/shard_map/ppermute | solution.py:16
  9.1 0.8 fusion.97
  10.4 4.6 %collective-permute-start.3 = (f32[4,2,66,1]{3,1,0,2:T(2,128)S(1)}, f32[4,2,66,1]{3,1,0,2:T(2,128)S(1)}, u32[]{:S(2)}, u32[]{:S(2)}) collective-permute-start(f32[4,2,66,1]{3,1,0,2:T(2,128)S(1)} %get-tuple-element.85), channel_id=1, source_target_pairs={{0,4},{4,8},{8,12},{12,16},{16,20},{20,24},{24,28},{1,5},{5,9},{9,... | collective-permute-start | bytes 6344 | tf_op jit(solution)/shard_map/ppermute | solution.py:16
  15.0 5.6 %collective-permute-start.2 = (f32[4,2,66,1]{3,1,0,2:T(2,128)S(1)}, f32[4,2,66,1]{3,1,0,2:T(2,128)S(1)}, u32[]{:S(2)}, u32[]{:S(2)}) collective-permute-start(f32[4,2,66,1]{3,1,0,2:T(2,128)S(1)} %get-tuple-element.84), channel_id=1, source_target_pairs={{4,0},{8,4},{12,8},{16,12},{20,16},{24,20},{28,24},{5,1},{9,5},{13... | collective-permute-start | bytes 6344 | tf_op jit(solution)/shard_map/ppermute | solution.py:17
  22.1 0.8 fusion.127
  23.0 0.8 fusion.126
  26.3 1.1 fusion.91
  28.0 1.3 %constant_dynamic-update-slice_fusion.20 = f32[10,2,2,64]{3,2,1,0:T(2,128)} fusion(f32[2,2,64,1]{2,1,0,3:T(2,128)} %copy.909), kind=kLoop, calls=%fused_computation.202 | loop fusion | bytes 3072
  30.7 0.9 pad_maximum_fusion
  32.0 1.6 %collective-permute-start.5 = (f32[4,1,66,130]{3,1,0,2:T(1,128)S(1)}, f32[4,1,66,130]{3,1,0,2:T(1,128)S(1)}, u32[]{:S(2)}, u32[]{:S(2)}) collective-permute-start(f32[4,1,66,130]{3,1,0,2:T(1,128)S(1)} %get-tuple-element.76), channel_id=1, source_target_pairs={{0,1},{1,2},{2,3},{4,5},{5,6},{6,7},{8,9},{9,10},{10,11},{12,13},{... | collective-permute-start | bytes 411848 | tf_op jit(solution)/shard_map/ppermute | solution.py:16
  33.7 1.5 %collective-permute-start.4 = (f32[4,1,66,130]{3,1,0,2:T(1,128)S(1)}, f32[4,1,66,130]{3,1,0,2:T(1,128)S(1)}, u32[]{:S(2)}, u32[]{:S(2)}) collective-permute-start(f32[4,1,66,130]{3,1,0,2:T(1,128)S(1)} %get-tuple-element.75), channel_id=1, source_target_pairs={{1,0},{2,1},{3,2},{5,4},{6,5},{7,6},{9,8},{10,9},{11,10},{13,12},{... | collective-permute-start | bytes 411848 | tf_op jit(solution)/shard_map/ppermute | solution.py:17
  35.7 0.9 fusion.94
  36.9 0.8 fusion.92
  39.2 4.1 %collective-permute-done.4 = f32[4,1,66,130]{3,1,0,2:T(1,128)S(1)} collective-permute-done((f32[4,1,66,130]{3,1,0,2:T(1,128)S(1)}, f32[4,1,66,130]{3,1,0,2:T(1,128)S(1)}, u32[]{:S(2)}, u32[]{:S(2)}) %collective-permute-start.4) | collective-permute-done | bytes 137312 | tf_op jit(solution)/shard_map/ppermute | solution.py:17
  43.9 0.8 fusion.23
  52.0 29.3 %all-gather = f32[160,2,2,128]{3,2,1,0:T(2,128)S(1)} all-gather(f32[10,2,2,128]{3,2,1,0:T(2,128)S(1)} %constant_dynamic-update-slice_fusion.1), channel_id=2, replica_groups=mesh['gx'=16,'gy'=8,'gz'=4] {'gx'}, dimensions={0}, use_global_device_ids=true | all-gather | bytes 348160 | tf_op jit(solution)/shard_map/all_gather | solution.py:192
  83.9 0.8 multiply_subtract_fusion.4
  86.2 0.8 multiply_subtract_fusion.3
  88.5 0.8 multiply_subtract_fusion.2
  90.8 0.8 multiply_subtract_fusion.1
  93.0 0.8 multiply_subtract_fusion
  99.8 22.8 %all-gather.1 = f32[80,2,2,64]{3,2,1,0:T(2,128)S(1)} all-gather(f32[10,2,2,64]{3,2,1,0:T(2,128)S(1)} %constant_dynamic-update-slice_fusion.11), channel_id=3, replica_groups=mesh['gx'=16,'gy'=8,'gz'=4] {'gy'}, dimensions={0}, use_global_device_ids=true | all-gather | bytes 92160 | tf_op jit(solution)/shard_map/all_gather | solution.py:196
  (250 shorter events, 34.7 us)
Async XLA Ops:
  0.0 1.0 copy-start.18
  1.2 6.3 %collective-permute-start = (f32[4,2,1,128]{3,1,0,2:T(2,128)S(1)}, f32[4,2,1,128]{3,1,0,2:T(2,128)S(1)}, u32[]{:S(2)}, u32[]{:S(2)}) collective-permute-start(f32[4,2,1,128]{3,1,0,2:T(2,128)S(1)} %get-tuple-element.105), channel_id=1, source_target_pairs={{32,0},{64,32},{96,64},{128,96},{160,128},{192,160},{224,192},{256... | collective-permute-start | bytes 12296 | tf_op jit(solution)/shard_map/ppermute | solution.py:17
  2.5 5.7 %collective-permute-start.1 = (f32[4,2,1,128]{3,1,0,2:T(2,128)S(1)}, f32[4,2,1,128]{3,1,0,2:T(2,128)S(1)}, u32[]{:S(2)}, u32[]{:S(2)}) collective-permute-start(f32[4,2,1,128]{3,1,0,2:T(2,128)S(1)} %get-tuple-element.104), channel_id=1, source_target_pairs={{0,32},{32,64},{64,96},{96,128},{128,160},{160,192},{192,224},{224... | collective-permute-start | bytes 12296 | tf_op jit(solution)/shard_map/ppermute | solution.py:16
  7.5 16.7 %copy-start.12 = (f32[4,2,1,128]{3,1,0,2:T(2,128)}, f32[4,2,1,128]{3,1,0,2:T(2,128)S(1)}, u32[]{:S(2)}) copy-start(f32[4,2,1,128]{3,1,0,2:T(2,128)S(1)} %collective-permute-done) | copy-start | bytes 12292
  8.2 16.0 %copy-start.15 = (f32[4,2,1,128]{3,1,0,2:T(2,128)}, f32[4,2,1,128]{3,1,0,2:T(2,128)S(1)}, u32[]{:S(2)}) copy-start(f32[4,2,1,128]{3,1,0,2:T(2,128)S(1)} %collective-permute-done.1) | copy-start | bytes 12292
  9.1 14.7 %copy-start.22 = (f32[2,2,1,128]{3,1,0,2:T(2,128)}, f32[2,2,1,128]{3,1,0,2:T(2,128)S(1)}, u32[]{:S(2)}) copy-start(f32[2,2,1,128]{3,1,0,2:T(2,128)S(1)} %get-tuple-element.345) | copy-start | bytes 6148
  10.4 13.5 %collective-permute-start.3 = (f32[4,2,66,1]{3,1,0,2:T(2,128)S(1)}, f32[4,2,66,1]{3,1,0,2:T(2,128)S(1)}, u32[]{:S(2)}, u32[]{:S(2)}) collective-permute-start(f32[4,2,66,1]{3,1,0,2:T(2,128)S(1)} %get-tuple-element.85), channel_id=1, source_target_pairs={{0,4},{4,8},{8,12},{12,16},{16,20},{20,24},{24,28},{1,5},{5,9},{9,... | collective-permute-start | bytes 6344 | tf_op jit(solution)/shard_map/ppermute | solution.py:16
  15.0 8.9 %collective-permute-start.2 = (f32[4,2,66,1]{3,1,0,2:T(2,128)S(1)}, f32[4,2,66,1]{3,1,0,2:T(2,128)S(1)}, u32[]{:S(2)}, u32[]{:S(2)}) collective-permute-start(f32[4,2,66,1]{3,1,0,2:T(2,128)S(1)} %get-tuple-element.84), channel_id=1, source_target_pairs={{4,0},{8,4},{12,8},{16,12},{20,16},{24,20},{28,24},{5,1},{9,5},{13... | collective-permute-start | bytes 6344 | tf_op jit(solution)/shard_map/ppermute | solution.py:17
  23.8 0.9 copy-start
  32.0 7.1 %collective-permute-start.5 = (f32[4,1,66,130]{3,1,0,2:T(1,128)S(1)}, f32[4,1,66,130]{3,1,0,2:T(1,128)S(1)}, u32[]{:S(2)}, u32[]{:S(2)}) collective-permute-start(f32[4,1,66,130]{3,1,0,2:T(1,128)S(1)} %get-tuple-element.76), channel_id=1, source_target_pairs={{0,1},{1,2},{2,3},{4,5},{5,6},{6,7},{8,9},{9,10},{10,11},{12,13},{... | collective-permute-start | bytes 411848 | tf_op jit(solution)/shard_map/ppermute | solution.py:16
  33.7 9.6 %collective-permute-start.4 = (f32[4,1,66,130]{3,1,0,2:T(1,128)S(1)}, f32[4,1,66,130]{3,1,0,2:T(1,128)S(1)}, u32[]{:S(2)}, u32[]{:S(2)}) collective-permute-start(f32[4,1,66,130]{3,1,0,2:T(1,128)S(1)} %get-tuple-element.75), channel_id=1, source_target_pairs={{1,0},{2,1},{3,2},{5,4},{6,5},{7,6},{9,8},{10,9},{11,10},{13,12},{... | collective-permute-start | bytes 411848 | tf_op jit(solution)/shard_map/ppermute | solution.py:17
  35.7 0.9 copy-start.1
  38.9 4.3 %copy-start.14 = (f32[4,2,1,128]{3,1,0,2:T(2,128)S(1)}, f32[4,2,1,128]{3,1,0,2:T(2,128)}, u32[]{:S(2)}) copy-start(f32[4,2,1,128]{3,1,0,2:T(2,128)} %copy-done.12) | copy-start | bytes 12292
  38.9 4.3 %copy-start.17 = (f32[4,2,1,128]{3,1,0,2:T(2,128)S(1)}, f32[4,2,1,128]{3,1,0,2:T(2,128)}, u32[]{:S(2)}) copy-start(f32[4,2,1,128]{3,1,0,2:T(2,128)} %copy-done.15) | copy-start | bytes 12292
  43.9 0.9 copy-start.19
  44.9 1.0 copy-start.11
  44.9 1.0 copy-start.8
  44.9 1.0 copy-start.9
  45.1 1.0 copy-start.6
  45.1 1.1 copy-start.7
  45.2 0.9 copy-start.23
  82.6 1.0 copy-start.4
  82.6 1.0 copy-start.5
  83.0 1.0 copy-start.2
  (8 other events, 6.2 us)
where the time goes:
time: 125 us
  blocking collectives  52.2 us (42%)
  local copies, waits for them, and re-layouts  29.3 us (23%)
  starting transfers between devices  19.6 us (16%)
  other arithmetic  17.7 us (14%)
  waiting for transfers between devices  4.98 us (4%)
    all_gather x1, blocking collectives, on_device(): gathered = lax.all_gather(pieces[None], 'gx', axis=0, tiled=True)  29.3 us
    all_gather x1, blocking collectives, on_device(): gathered = lax.all_gather(pieces[None], 'gy', axis=0, tiled=True)  22.8 us
    ppermute x3, starting transfers between devices, extended(): before = lax.ppermute(last, axis, up)  11.3 us
    unnamed x73, local copies, waits for them, and re-layouts  9.47 us
    sub x18, other arithmetic, cyclic_solve(): vector - ratio_low * shifted(vector, stride, axis_dim, 0.0, True)  8.43 us
    ppermute x3, starting transfers between devices, extended(): after = lax.ppermute(leading, axis, down)  8.35 us
    slice x44, local copies, waits for them, and re-layouts, shifted(): lax.slice_in_dim(values, stride, extent, axis=axis_dim)  7.24 us
    slice x60, local copies, waits for them, and re-layouts, shifted(): lax.slice_in_dim(values, 0, extent - stride, axis=axis_dim)  7 us
  transfers between devices with their start and end apart: 6, of which 3 were waited for; matrix products, arithmetic and copies ran while one was open for 6% of the time, Pallas kernels for 0%

commit v1 on v0

v1 whole, which is shorter than its diff:
```python
import jax
import jax.numpy as jnp
from jax import lax
from jax.experimental import pallas as pl
from jax.experimental.pallas import tpu as pltpu
from jax.sharding import PartitionSpec as P

F32 = jnp.float32
SUBS = 8


def struct(*shape):
    return jax.ShapeDtypeStruct(shape, F32)


def lane_index(shape):
    return lax.broadcasted_iota(jnp.int32, shape, len(shape) - 1)


def sub_index(shape):
    return lax.broadcasted_iota(jnp.int32, shape, len(shape) - 2)


def pack_kernel(v_ref, k_ref, up_ref, down_ref, edge_ref):
    lanes = v_ref.shape[-1]
    for f in range(2):
        up_ref[0, f] = v_ref[f, 1]
        up_ref[1, f] = k_ref[f, 1]
        down_ref[0, f] = v_ref[f, 0]
        down_ref[1, f] = k_ref[f, 0]
    lane = lane_index(v_ref.shape[2:])
    edge = jnp.zeros(v_ref.shape[2:], F32)
    for part, ref in enumerate((v_ref, k_ref)):
        for f in range(2):
            for z in range(2):
                m = part * 4 + f * 2 + z
                rows = ref[f, z]
                edge = jnp.where(lane == m, pltpu.roll(rows, (m + 1) % lanes, 1), edge)
                edge = jnp.where(lane == 8 + m, pltpu.roll(rows, 8 + m, 1), edge)
    edge_ref[...] = edge


def star_step(a, t, b, c, leak, hold=None):
    inv = 1.0 / (t + b + c)
    if hold is not None:
        inv = jnp.where(hold, 0.0, inv)
    to_first, to_next = t * inv, c * inv
    if hold is not None:
        to_next = jnp.where(hold, 1.0, to_next)
    return a + to_first * b, t * to_next, leak + to_next * b, inv, to_first, to_next


def factor(load, count, rows, scale, inner_ref, outer_ref, port_ref, work):
    for c in range(count):
        kappa = [load(c, k) for k in range(rows)]
        below = pltpu.roll(kappa[0], SUBS - 1, 0)
        face = [
            0.5 * scale * (kappa[k] + (kappa[k + 1] if k + 1 < rows else below)) for k in range(rows)
        ]
        hold = sub_index(kappa[0].shape) == SUBS - 1
        one = jnp.ones_like(kappa[0])
        a, t, b = one, face[0], one
        for k in range(1, rows):
            last = k == rows - 1
            a, t, b, inv, first, nxt = star_step(
                a, t, b, face[k], 0.0 if last else 1.0, hold if last else None
            )
            inner_ref[0, c, k - 1] = inv
            inner_ref[1, c, k - 1] = first
            inner_ref[2, c, k - 1] = nxt
        for number, values in enumerate((a, t, b)):
            work[number, pl.ds(c * SUBS, SUBS)] = values
        port_ref[3, pl.ds(c, 1)] = kappa[0][:1]
        port_ref[4, pl.ds(c, 1)] = kappa[rows - 1][SUBS - 1 :]

    def row(number, j):
        return work[number, pl.ds(j, count, stride=SUBS)]

    a, t, b = row(0, 0), row(1, 0), row(2, 0) + row(0, 1)
    for j in range(1, SUBS):
        leak = row(2, j) + (row(0, j + 1) if j + 1 < SUBS else 0.0)
        a, t, b, inv, first, nxt = star_step(a, t, b, row(1, j), leak)
        outer_ref[0, j - 1] = inv
        outer_ref[1, j - 1] = first
        outer_ref[2, j - 1] = nxt
    port_ref[0], port_ref[1], port_ref[2] = a, t, b


def matrix_kernel(k_ref, xi_ref, xo_ref, xp_ref, yi_ref, yo_ref, yp_ref, work, turned):
    scale = float(2 * k_ref.shape[2] * k_ref.shape[2])
    rows_x = k_ref.shape[2] // SUBS
    rows_y = k_ref.shape[3] // SUBS
    factor(
        lambda c, k: k_ref[c // 2, c % 2, pl.ds(k, SUBS, stride=rows_x)],
        4, rows_x, scale, xi_ref, xo_ref, xp_ref, work,
    )
    for f in range(2):
        turned[f] = k_ref[f].reshape(128, 128).T
    factor(
        lambda c, k: turned[c, pl.ds(k, SUBS, stride=rows_y)],
        2, rows_y, scale, yi_ref, yo_ref, yp_ref, work,
    )


def reduce_sources(load, count, rows, inner_ref, outer_ref, part_ref, outer_part_ref, work):
    for c in range(count):
        head, cur = load(c, 0), load(c, 1)
        for k in range(1, rows):
            part_ref[c, k - 1] = cur * inner_ref[0, c, k - 1]
            head = head + inner_ref[1, c, k - 1] * cur
            carried = inner_ref[2, c, k - 1] * cur
            cur = load(c, k + 1) + carried if k + 1 < rows else carried
        work[0, pl.ds(c * SUBS, SUBS)] = head
        work[1, pl.ds(c * SUBS, SUBS)] = cur

    def row(number, j):
        return work[number, pl.ds(j, count, stride=SUBS)]

    head, cur = row(0, 0), row(0, 1) + row(1, 0)
    for j in range(1, SUBS):
        outer_part_ref[j - 1] = cur * outer_ref[0, j - 1]
        head = head + outer_ref[1, j - 1] * cur
        carried = outer_ref[2, j - 1] * cur
        cur = row(1, j) + (row(0, j + 1) if j + 1 < SUBS else 0.0) + carried
    return head, cur


def send(pieces_ref, port_ref, head, tail):
    for d in range(pieces_ref.shape[0]):
        for q in range(5):
            pieces_ref[d, q] = port_ref[q]
        pieces_ref[d, 5] = head
        pieces_ref[d, 6] = tail


def ends(pieces_ref, me, scale):
    blocks = pieces_ref.shape[0]

    def piece(j):
        return [pieces_ref[j, q] for q in range(7)]

    half = 0.5 * scale

    def through(leak, source, near, t, far, near_src, far_src, face):
        x = leak + near
        xt = x + t
        total = far * xt + t * x
        q = face / (total + face * xt)
        return total * q, q * (xt * far_src + t * (source + near_src))

    left_leak = half * pieces_ref[0, 3]
    left_src = jnp.zeros_like(left_leak)
    right_leak = half * pieces_ref[blocks - 1, 4]
    right_src = jnp.zeros_like(right_leak)
    for step in range(blocks - 1):
        a, t, b, k_first, k_last, r_first, r_last = piece(step)
        face = half * (k_last + pieces_ref[step + 1, 3])
        leak, src = through(left_leak, left_src, a, t, b, r_first, r_last, face)
        left_leak = jnp.where(step < me, leak, left_leak)
        left_src = jnp.where(step < me, src, left_src)
        j = blocks - 1 - step
        a, t, b, k_first, k_last, r_first, r_last = piece(j)
        face = half * (k_first + pieces_ref[j - 1, 4])
        leak, src = through(right_leak, right_src, b, t, a, r_last, r_first, face)
        right_leak = jnp.where(j > me, leak, right_leak)
        right_src = jnp.where(j > me, src, right_src)
    a, t, b = (pieces_ref[me, q] for q in range(3))
    first = a + left_leak
    last = b + right_leak
    r_first = pieces_ref[me, 5] + left_src
    r_last = pieces_ref[me, 6] + right_src
    inv = 1.0 / (first * last + t * (first + last))
    return inv * ((last + t) * r_first + t * r_last), inv * (t * r_first + (first + t) * r_last)


def expand(x_first, x_last, count, rows, inner_ref, outer_ref, part_ref, outer_part_ref, work, store):
    def put(number, j, values):
        work[number, pl.ds(j, count, stride=SUBS)] = values

    put(0, 0, x_first)
    put(1, SUBS - 1, x_last)
    cur = x_last
    for j in range(SUBS - 1, 0, -1):
        cur = outer_part_ref[j - 1] + outer_ref[1, j - 1] * x_first + outer_ref[2, j - 1] * cur
        put(0, j, cur)
        put(1, j - 1, cur)
    for c in range(count):
        head = work[0, pl.ds(c * SUBS, SUBS)]
        cur = work[1, pl.ds(c * SUBS, SUBS)]
        for k in range(rows - 1, 0, -1):
            cur = part_ref[c, k - 1] + inner_ref[1, c, k - 1] * head + inner_ref[2, c, k - 1] * cur
            store(c, k, cur)
        store(c, 0, head)


def source_kernel(
    v_ref, k_ref, s_ref, below_ref, above_ref, left_ref, right_ref,
    xi_ref, xo_ref, xp_ref, pieces_ref, part_ref, outer_part_ref, work,
):
    lanes = v_ref.shape[3]
    rows = v_ref.shape[2] // SUBS
    along = float(4 * v_ref.shape[2] * v_ref.shape[2])
    vertical = 256.0
    lane = lane_index((SUBS, lanes))

    def load(c, k):
        f, z = divmod(c, 2)
        at = pl.ds(k, SUBS, stride=rows)
        v, kap = v_ref[f, z, at], k_ref[f, z, at]
        left, right = left_ref[at], right_ref[at]
        v_next = jnp.where(lane == lanes - 1, pltpu.roll(right, lanes - 9 - c, 1), pltpu.roll(v, lanes - 1, 1))
        k_next = jnp.where(lane == lanes - 1, pltpu.roll(right, lanes - 13 - c, 1), pltpu.roll(kap, lanes - 1, 1))
        upper = (0.5 * along) * (kap + k_next) * (v_next - v)
        v_left = pltpu.roll(left, (lanes - c) % lanes, 1)
        k_left = pltpu.roll(left, lanes - 4 - c, 1)
        first = (0.5 * along) * (kap + k_left) * (v - v_left)
        lower = jnp.where(lane == 0, first, pltpu.roll(upper, 1, 1))
        if z == 0:
            v_up, k_up = v_ref[f, 1, at], k_ref[f, 1, at]
            v_dn, k_dn = below_ref[0, f, at], below_ref[1, f, at]
        else:
            v_up, k_up = above_ref[0, f, at], above_ref[1, f, at]
            v_dn, k_dn = v_ref[f, 0, at], k_ref[f, 0, at]
        layers = (0.5 * vertical) * ((kap + k_up) * (v_up - v) - (kap + k_dn) * (v - v_dn))
        return (upper - lower) + layers + (2.0 * v + s_ref[f, z, at])

    head, tail = reduce_sources(load, 4, rows, xi_ref, xo_ref, part_ref, outer_part_ref, work)
    send(pieces_ref, xp_ref, head, tail)


def middle_kernel(
    me_ref, pieces_ref, v_ref, xi_ref, xo_ref, part_ref, outer_part_ref, yi_ref, yo_ref, yp_ref,
    out_pieces_ref, y_part_ref, y_outer_part_ref, work, swept, turned,
):
    scale = float(2 * v_ref.shape[2] * v_ref.shape[2])
    rows_x = v_ref.shape[2] // SUBS
    rows_y = v_ref.shape[3] // SUBS
    x_first, x_last = ends(pieces_ref, me_ref[0], scale)

    def store(c, k, values):
        f, z = divmod(c, 2)
        at = pl.ds(k, SUBS, stride=rows_x)
        swept[f, pl.ds(z * v_ref.shape[2] + k, SUBS, stride=rows_x)] = values - 2.0 * v_ref[f, z, at]

    expand(x_first, x_last, 4, rows_x, xi_ref, xo_ref, part_ref, outer_part_ref, work, store)
    for f in range(2):
        turned[f] = swept[f].T
    head, tail = reduce_sources(
        lambda c, k: turned[c, pl.ds(k, SUBS, stride=rows_y)],
        2, rows_y, yi_ref, yo_ref, y_part_ref, y_outer_part_ref, work,
    )
    send(out_pieces_ref, yp_ref, head, tail)


def last_kernel(me_ref, pieces_ref, v_ref, yi_ref, yo_ref, part_ref, outer_part_ref, out_ref, work, turned):
    scale = float(2 * v_ref.shape[2] * v_ref.shape[2])
    rows_y = v_ref.shape[3] // SUBS
    x_first, x_last = ends(pieces_ref, me_ref[0], scale)

    def store(c, k, values):
        turned[c, pl.ds(k, SUBS, stride=rows_y)] = values

    expand(x_first, x_last, 2, rows_y, yi_ref, yo_ref, part_ref, outer_part_ref, work, store)
    for f in range(2):
        out_ref[f] = v_ref[f] + turned[f].T.reshape(v_ref.shape[1:])


def call(kernel, outs, scratch, *args, scalars=0):
    smem = pl.BlockSpec(memory_space=pltpu.SMEM)
    vmem = pl.BlockSpec(memory_space=pltpu.VMEM)
    return pl.pallas_call(
        kernel,
        out_shape=outs,
        in_specs=[smem] * scalars + [vmem] * (len(args) - scalars),
        out_specs=[vmem] * len(outs),
        scratch_shapes=[pltpu.VMEM(shape, F32) for shape in scratch],
        compiler_params=pltpu.CompilerParams(vmem_limit_bytes=24 * 1024 * 1024),
    )(*args)


def shift(values, axis, step):
    peers = lax.axis_size(axis)
    return lax.ppermute(
        values, axis, [(i, i + step) for i in range(peers) if 0 <= i + step < peers]
    )


def on_device(v, kappa, source):
    _, _, nx, ny = v.shape
    rows_x, rows_y = nx // SUBS, ny // SUBS
    gx, gy = lax.axis_size("gx"), lax.axis_size("gy")
    up, down, edge = call(
        pack_kernel, [struct(2, 2, nx, ny), struct(2, 2, nx, ny), struct(nx, ny)], [], v, kappa
    )
    left = shift(edge, "gy", 1)
    right = shift(edge, "gy", -1)
    below = shift(up, "gz", 1)
    above = shift(down, "gz", -1)
    xi, xo, xp, yi, yo, yp = call(
        matrix_kernel,
        [
            struct(3, 4, rows_x - 1, SUBS, ny), struct(3, SUBS - 1, 4, ny), struct(5, 4, ny),
            struct(3, 2, rows_y - 1, SUBS, 128), struct(3, SUBS - 1, 2, 128), struct(5, 2, 128),
        ],
        [(3, 4 * SUBS, 128), (2, 128, 128)],
        kappa,
    )
    pieces, x_part, x_outer = call(
        source_kernel,
        [struct(gx, 7, 4, ny), struct(4, rows_x - 1, SUBS, ny), struct(SUBS - 1, 4, ny)],
        [(2, 4 * SUBS, 128)],
        v, kappa, source, below, above, left, right, xi, xo, xp,
    )
    pieces = lax.all_to_all(pieces, "gx", 0, 0)
    me = lax.axis_index("gx").astype(jnp.int32).reshape(1)
    pieces, y_part, y_outer = call(
        middle_kernel,
        [struct(gy, 7, 2, 128), struct(2, rows_y - 1, SUBS, 128), struct(SUBS - 1, 2, 128)],
        [(2, 4 * SUBS, 128), (2, 128, 128), (2, 128, 128)],
        me, pieces, v, xi, xo, x_part, x_outer, yi, yo, yp,
        scalars=1,
    )
    pieces = lax.all_to_all(pieces, "gy", 0, 0)
    me = lax.axis_index("gy").astype(jnp.int32).reshape(1)
    (out,) = call(
        last_kernel,
        [struct(*v.shape)],
        [(2, 4 * SUBS, 128), (2, 128, 128)],
        me, pieces, v, yi, yo, y_part, y_outer,
        scalars=1,
    )
    return out


def solution(mesh):
    spec = P(None, "gz", "gx", "gy")
    return jax.shard_map(
        on_device, mesh=mesh, in_specs=(spec, spec, spec), out_specs=spec, check_vma=False
    )
```

time: 125 us -> 62 us (0.50)
  the two profiles are of different devices: /device:TPU:1 before, /device:TPU:56 now
where the time goes in v1:
time: 62 us; the launch traced here: 61.6 us
  starting transfers between devices  29.6 us (48%)
  waiting for transfers between devices  26 us (42%)
  Pallas kernels  4.12 us (7%)
  local copies, waits for them, and re-layouts  1.82 us (3%)
    all_to_all x1, waiting for transfers between devices, on_device(): pieces = lax.all_to_all(pieces, 'gx', 0, 0)  17.3 us
    all_to_all x1, starting transfers between devices, on_device(): pieces = lax.all_to_all(pieces, 'gx', 0, 0)  15.2 us
    ppermute x4, starting transfers between devices, shift(): lax.ppermute(values, axis, [(i, i + step) for i in range(peers) if 0 <= i...  8.56 us
    all_to_all x1, starting transfers between devices, on_device(): pieces = lax.all_to_all(pieces, 'gy', 0, 0)  5.79 us
    all_to_all x1, waiting for transfers between devices, on_device(): pieces = lax.all_to_all(pieces, 'gy', 0, 0)  5.58 us
    pallas_call x5, Pallas kernels, call(): pl.pallas_call(kernel, out_shape=outs, in_specs=[smem] * scalars + [vmem]...  4.12 us
    ppermute x4, waiting for transfers between devices, shift(): lax.ppermute(values, axis, [(i, i + step) for i in range(peers) if 0 <= i...  3.16 us
    unnamed x8, local copies, waits for them, and re-layouts  1.82 us
  transfers between devices with their start and end apart: 6, of which 3 were waited for; matrix products, arithmetic and copies ran while one was open for 0% of the time, Pallas kernels for 1%

profile of v1, /device:TPU:56, one launch (start us, length us, event | category | flops | bytes accessed | tf_op | source)
XLA Modules:
  0.0 61.6 jit_solution(1606432539764440615)
XLA Ops:
  0.0 0.0 copy-start
  0.0 0.9 %copy-done = f32[2,2,64,128]{3,2,1,0:T(8,128)S(1)} copy-done((f32[2,2,64,128]{3,2,1,0:T(8,128)S(1)}, f32[2,2,64,128]{3,2,1,0:T(8,128)}, u32[]{:S(2)}) %copy-start) | copy-done | bytes 131096
  0.9 0.0 copy-start.2
  0.9 0.9 %copy-done.2 = f32[2,2,64,128]{3,2,1,0:T(8,128)S(1)} copy-done((f32[2,2,64,128]{3,2,1,0:T(8,128)S(1)}, f32[2,2,64,128]{3,2,1,0:T(8,128)}, u32[]{:S(2)}) %copy-start.2) | copy-done | bytes 131096
  1.8 0.2 shard_map.37
  2.0 0.0 copy-start.1
  2.0 1.4 %collective-permute-start = (f32[2,2,64,128]{3,2,1,0:T(8,128)S(1)}, f32[2,2,64,128]{3,2,1,0:T(8,128)S(1)}, u32[]{:S(2)}, u32[]{:S(2)}) collective-permute-start(f32[2,2,64,128]{3,2,1,0:T(8,128)S(1)} %get-tuple-element.20), channel_id=1, source_target_pairs={{0,1},{1,2},{2,3},{4,5},{5,6},{6,7},{8,9},{9,10},{10,11},{12,13},{... | collective-permute-start | bytes 393224 | tf_op jit(solution)/shard_map/ppermute | solution.py:283
  3.5 4.6 %collective-permute-start.1 = (f32[2,2,64,128]{3,2,1,0:T(8,128)S(1)}, f32[2,2,64,128]{3,2,1,0:T(8,128)S(1)}, u32[]{:S(2)}, u32[]{:S(2)}) collective-permute-start(f32[2,2,64,128]{3,2,1,0:T(8,128)S(1)} %get-tuple-element.21), channel_id=1, source_target_pairs={{1,0},{2,1},{3,2},{5,4},{6,5},{7,6},{9,8},{10,9},{11,10},{13,12},{... | collective-permute-start | bytes 393224 | tf_op jit(solution)/shard_map/ppermute | solution.py:283
  8.0 1.3 %collective-permute-start.2 = (f32[64,128]{1,0:T(8,128)S(1)}, f32[64,128]{1,0:T(8,128)S(1)}, u32[]{:S(2)}, u32[]{:S(2)}) collective-permute-start(f32[64,128]{1,0:T(8,128)S(1)} %get-tuple-element.22), channel_id=1, source_target_pairs={{0,4},{4,8},{8,12},{12,16},{16,20},{20,24},{24,28},{1,5},{5,9},{9,... | collective-permute-start | bytes 98312 | tf_op jit(solution)/shard_map/ppermute | solution.py:283
  9.3 1.3 %collective-permute-start.3 = (f32[64,128]{1,0:T(8,128)S(1)}, f32[64,128]{1,0:T(8,128)S(1)}, u32[]{:S(2)}, u32[]{:S(2)}) collective-permute-start(f32[64,128]{1,0:T(8,128)S(1)} %get-tuple-element.22), channel_id=1, source_target_pairs={{4,0},{8,4},{12,8},{16,12},{20,16},{24,20},{28,24},{5,1},{9,5},{13... | collective-permute-start | bytes 98312 | tf_op jit(solution)/shard_map/ppermute | solution.py:283
  10.6 0.4 shard_map.38
  11.0 0.0 collective-permute-done.2.left_ref
  11.0 3.1 %collective-permute-done.3.right_ref = f32[64,128]{1,0:T(8,128)S(1)} collective-permute-done((f32[64,128]{1,0:T(8,128)S(1)}, f32[64,128]{1,0:T(8,128)S(1)}, u32[]{:S(2)}, u32[]{:S(2)}) %collective-permute-start.3) | collective-permute-done | bytes 32800 | tf_op jit(solution)/shard_map/ppermute | solution.py:283
  14.1 0.0 collective-permute-done.below_ref
  14.1 0.0 collective-permute-done.1.above_ref
  14.2 0.0 copy-done.3
  14.2 0.0 copy-done.1
  14.2 1.5 %shard_map.39 = (f32[16,7,4,128]{3,2,1,0:T(4,128)}, f32[4,7,8,128]{3,2,1,0:T(8,128)S(1)}, f32[7,4,128]{2,1,0:T(4,128)S(1)}) custom-call(f32[2,2,64,128]{3,2,1,0:T(8,128)S(1)} %copy-done.1, f32[2,2,64,128]{3,2,1,0:T(8,128)S(1)} %copy-done.2, f32[2,2,64,128]{3,2,1,0:T(8,128)S(1)} %copy-done.3, f32[2,2,64,128]{3,2,1,0:T(8,128)S(1)} %collective-permute-done.below_ref, ...), custom_call_target="tpu_custom_call" | custom-call | tf_op jit(solution)/shard_map/pallas_call | solution.py:271
  15.7 15.2 %all-to-all-start = ((f32[16,7,4,128]{3,2,1,0:T(4,128)}), f32[16,7,4,128]{3,2,1,0:T(4,128)S(1)}, u32[]{:S(2)}, u32[]{:S(2)}) async-start(f32[16,7,4,128]{3,2,1,0:T(4,128)} %get-tuple-element.26), calls=%async_computation | async-start | bytes 458752 | tf_op jit(solution)/shard_map/all_to_all | solution.py:314
  30.9 17.3 %all-to-all-done.pieces_ref = f32[16,7,4,128]{3,2,1,0:T(4,128)S(1)} async-done(((f32[16,7,4,128]{3,2,1,0:T(4,128)}), f32[16,7,4,128]{3,2,1,0:T(4,128)S(1)}, u32[]{:S(2)}, u32[]{:S(2)}) %all-to-all-start) | async-done | bytes 229408 | tf_op jit(solution)/shard_map/all_to_all | solution.py:314
  48.2 1.1 %shard_map.40 = (f32[8,7,2,128]{3,2,1,0:T(2,128)}, f32[2,15,8,128]{3,2,1,0:T(8,128)S(1)}, f32[7,2,128]{2,1,0:T(2,128)S(1)}) custom-call(s32[1]{0:T(128)} %bitcast.1.me_ref, f32[16,7,4,128]{3,2,1,0:T(4,128)S(1)} %all-to-all-done.pieces_ref, f32[2,2,64,128]{3,2,1,0:T(8,128)S(1)} %copy-done.1, f32[3,4,7,8,128]{4,3,2,1,0:T(8,128)S(1)} %get-tuple-element.23.xi_ref, ...), custom_call_target="tpu_custom_call" | custom-call | tf_op jit(solution)/shard_map/pallas_call | solution.py:271
  49.3 5.8 %all-to-all-start.1 = ((f32[8,7,2,128]{3,2,1,0:T(2,128)}), f32[8,7,2,128]{3,2,1,0:T(2,128)S(1)}, u32[]{:S(2)}, u32[]{:S(2)}) async-start(f32[8,7,2,128]{3,2,1,0:T(2,128)} %get-tuple-element.32), calls=%async_computation.1 | async-start | bytes 114688 | tf_op jit(solution)/shard_map/all_to_all | solution.py:323
  55.1 5.6 %all-to-all-done.1.pieces_ref = f32[8,7,2,128]{3,2,1,0:T(2,128)S(1)} async-done(((f32[8,7,2,128]{3,2,1,0:T(2,128)}), f32[8,7,2,128]{3,2,1,0:T(2,128)S(1)}, u32[]{:S(2)}, u32[]{:S(2)}) %all-to-all-start.1) | async-done | bytes 57376 | tf_op jit(solution)/shard_map/all_to_all | solution.py:323
  60.7 0.9 %shard_map.41 = f32[2,2,64,128]{3,2,1,0:T(8,128)} custom-call(s32[1]{0:T(128)} %bitcast.me_ref, f32[8,7,2,128]{3,2,1,0:T(2,128)S(1)} %all-to-all-done.1.pieces_ref, f32[2,2,64,128]{3,2,1,0:T(8,128)S(1)} %copy-done.1, f32[3,2,15,8,128]{4,3,2,1,0:T(8,128)S(1)} %get-tuple-element.29.yi_ref, f32[3,7,2,128]{3,2,1,0:T(2,128)S(1)} %get-tuple-element.30.yo_ref, ...), custom_call_target="tpu_custom_call" | custom-call | tf_op jit(solution)/shard_map/pallas_call | solution.py:271
  (1 shorter events, 0.0 us)
Async XLA Ops:
  0.0 0.9 %copy-start = (f32[2,2,64,128]{3,2,1,0:T(8,128)S(1)}, f32[2,2,64,128]{3,2,1,0:T(8,128)}, u32[]{:S(2)}) copy-start(f32[2,2,64,128]{3,2,1,0:T(8,128)} %v_ref.7) | copy-start | bytes 393220
  0.9 0.9 %copy-start.2 = (f32[2,2,64,128]{3,2,1,0:T(8,128)S(1)}, f32[2,2,64,128]{3,2,1,0:T(8,128)}, u32[]{:S(2)}) copy-start(f32[2,2,64,128]{3,2,1,0:T(8,128)} %k_ref.5) | copy-start | bytes 393220
  1.8 12.3 %copy-start.3 = (f32[2,2,64,128]{3,2,1,0:T(8,128)S(1)}, f32[2,2,64,128]{3,2,1,0:T(8,128)}, u32[]{:S(2)}) copy-start(f32[2,2,64,128]{3,2,1,0:T(8,128)} %s_ref.1) | copy-start | bytes 393220
  2.0 12.1 %copy-start.1 = (f32[2,2,64,128]{3,2,1,0:T(8,128)S(1)}, f32[2,2,64,128]{3,2,1,0:T(8,128)}, u32[]{:S(2)}) copy-start(f32[2,2,64,128]{3,2,1,0:T(8,128)} %v_ref.7) | copy-start | bytes 393220
  2.0 12.1 %collective-permute-start = (f32[2,2,64,128]{3,2,1,0:T(8,128)S(1)}, f32[2,2,64,128]{3,2,1,0:T(8,128)S(1)}, u32[]{:S(2)}, u32[]{:S(2)}) collective-permute-start(f32[2,2,64,128]{3,2,1,0:T(8,128)S(1)} %get-tuple-element.20), channel_id=1, source_target_pairs={{0,1},{1,2},{2,3},{4,5},{5,6},{6,7},{8,9},{9,10},{10,11},{12,13},{... | collective-permute-start | bytes 393224 | tf_op jit(solution)/shard_map/ppermute | solution.py:283
  3.5 10.7 %collective-permute-start.1 = (f32[2,2,64,128]{3,2,1,0:T(8,128)S(1)}, f32[2,2,64,128]{3,2,1,0:T(8,128)S(1)}, u32[]{:S(2)}, u32[]{:S(2)}) collective-permute-start(f32[2,2,64,128]{3,2,1,0:T(8,128)S(1)} %get-tuple-element.21), channel_id=1, source_target_pairs={{1,0},{2,1},{3,2},{5,4},{6,5},{7,6},{9,8},{10,9},{11,10},{13,12},{... | collective-permute-start | bytes 393224 | tf_op jit(solution)/shard_map/ppermute | solution.py:283
  8.0 3.0 %collective-permute-start.2 = (f32[64,128]{1,0:T(8,128)S(1)}, f32[64,128]{1,0:T(8,128)S(1)}, u32[]{:S(2)}, u32[]{:S(2)}) collective-permute-start(f32[64,128]{1,0:T(8,128)S(1)} %get-tuple-element.22), channel_id=1, source_target_pairs={{0,4},{4,8},{8,12},{12,16},{16,20},{20,24},{24,28},{1,5},{5,9},{9,... | collective-permute-start | bytes 98312 | tf_op jit(solution)/shard_map/ppermute | solution.py:283
  9.3 4.8 %collective-permute-start.3 = (f32[64,128]{1,0:T(8,128)S(1)}, f32[64,128]{1,0:T(8,128)S(1)}, u32[]{:S(2)}, u32[]{:S(2)}) collective-permute-start(f32[64,128]{1,0:T(8,128)S(1)} %get-tuple-element.22), channel_id=1, source_target_pairs={{4,0},{8,4},{12,8},{16,12},{20,16},{24,20},{28,24},{5,1},{9,5},{13... | collective-permute-start | bytes 98312 | tf_op jit(solution)/shard_map/ppermute | solution.py:283
  15.7 32.5 %all-to-all-start = ((f32[16,7,4,128]{3,2,1,0:T(4,128)}), f32[16,7,4,128]{3,2,1,0:T(4,128)S(1)}, u32[]{:S(2)}, u32[]{:S(2)}) async-start(f32[16,7,4,128]{3,2,1,0:T(4,128)} %get-tuple-element.26), calls=%async_computation | async-start | bytes 458752 | tf_op jit(solution)/shard_map/all_to_all | solution.py:314
  49.3 11.4 %all-to-all-start.1 = ((f32[8,7,2,128]{3,2,1,0:T(2,128)}), f32[8,7,2,128]{3,2,1,0:T(2,128)S(1)}, u32[]{:S(2)}, u32[]{:S(2)}) async-start(f32[8,7,2,128]{3,2,1,0:T(2,128)} %get-tuple-element.32), calls=%async_computation.1 | async-start | bytes 114688 | tf_op jit(solution)/shard_map/all_to_all | solution.py:323

commit v2 on v1

--- a/solution.py
+++ b/solution.py
@@ -6,6 +6,7 @@
 from jax.sharding import PartitionSpec as P
 
 F32 = jnp.float32
+VERTICAL = 256.0
 SUBS = 8
 
 
@@ -21,20 +22,24 @@
     return lax.broadcasted_iota(jnp.int32, shape, len(shape) - 2)
 
 
-def pack_kernel(v_ref, k_ref, up_ref, down_ref, edge_ref):
-    lanes = v_ref.shape[-1]
-    for f in range(2):
-        up_ref[0, f] = v_ref[f, 1]
-        up_ref[1, f] = k_ref[f, 1]
-        down_ref[0, f] = v_ref[f, 0]
-        down_ref[1, f] = k_ref[f, 0]
-    lane = lane_index(v_ref.shape[2:])
-    edge = jnp.zeros(v_ref.shape[2:], F32)
-    for part, ref in enumerate((v_ref, k_ref)):
+def pack_kernel(v_hbm, k_hbm, up_ref, down_ref, edge_ref, sems):
+    copies = [
+        pltpu.make_async_copy(src.at[:, z], dst.at[part], sems.at[z, part])
+        for z, dst in ((1, up_ref), (0, down_ref))
+        for part, src in enumerate((v_hbm, k_hbm))
+    ]
+    for copy in copies:
+        copy.start()
+    for copy in copies:
+        copy.wait()
+    lanes = up_ref.shape[-1]
+    lane = lane_index(up_ref.shape[2:])
+    edge = jnp.zeros(up_ref.shape[2:], F32)
+    for part in range(2):
         for f in range(2):
-            for z in range(2):
+            for z, ref in enumerate((down_ref, up_ref)):
                 m = part * 4 + f * 2 + z
-                rows = ref[f, z]
+                rows = ref[part, f]
                 edge = jnp.where(lane == m, pltpu.roll(rows, (m + 1) % lanes, 1), edge)
                 edge = jnp.where(lane == 8 + m, pltpu.roll(rows, 8 + m, 1), edge)
     edge_ref[...] = edge
@@ -86,16 +91,35 @@
     port_ref[0], port_ref[1], port_ref[2] = a, t, b
 
 
-def matrix_kernel(k_ref, xi_ref, xo_ref, xp_ref, yi_ref, yo_ref, yp_ref, work, turned):
-    scale = float(2 * k_ref.shape[2] * k_ref.shape[2])
-    rows_x = k_ref.shape[2] // SUBS
-    rows_y = k_ref.shape[3] // SUBS
+def local_kernel(
+    down_ref, up_ref, s_ref, xi_ref, xo_ref, xp_ref, yi_ref, yo_ref, yp_ref, local_ref, work, turned
+):
+    _, _, nx, lanes = down_ref.shape
+    scale = float(2 * nx * nx)
+    rows_x = nx // SUBS
+    rows_y = lanes // SUBS
+    layers = (down_ref, up_ref)
+    lane = lane_index((SUBS, lanes))
+    for f in range(2):
+        for k in range(rows_x):
+            at = pl.ds(k, SUBS, stride=rows_x)
+            v = [ref[0, f, at] for ref in layers]
+            kap = [ref[1, f, at] for ref in layers]
+            between = (0.5 * VERTICAL) * (kap[0] + kap[1]) * (v[1] - v[0])
+            for z in range(2):
+                v_next = pltpu.roll(v[z], lanes - 1, 1)
+                k_next = pltpu.roll(kap[z], lanes - 1, 1)
+                upper = scale * (kap[z] + k_next) * (v_next - v[z])
+                upper = jnp.where(lane == lanes - 1, 0.0, upper)
+                along = upper - pltpu.roll(upper, 1, 1)
+                local_ref[f * 2 + z, k] = along + (between if z == 0 else -between) + (2.0 * v[z] + s_ref[f, z, at])
     factor(
-        lambda c, k: k_ref[c // 2, c % 2, pl.ds(k, SUBS, stride=rows_x)],
+        lambda c, k: layers[c % 2][1, c // 2, pl.ds(k, SUBS, stride=rows_x)],
         4, rows_x, scale, xi_ref, xo_ref, xp_ref, work,
     )
     for f in range(2):
-        turned[f] = k_ref[f].reshape(128, 128).T
+        both = jnp.concatenate([down_ref[1, f], up_ref[1, f]], 0)
+        turned[f] = both.T
     factor(
         lambda c, k: turned[c, pl.ds(k, SUBS, stride=rows_y)],
         2, rows_y, scale, yi_ref, yo_ref, yp_ref, work,
@@ -194,53 +218,54 @@
 
 
 def source_kernel(
-    v_ref, k_ref, s_ref, below_ref, above_ref, left_ref, right_ref,
-    xi_ref, xo_ref, xp_ref, pieces_ref, part_ref, outer_part_ref, work,
+    down_ref, up_ref, local_ref, below_ref, above_ref, edge_ref, chip_ref, link_ref,
+    xi_ref, xo_ref, xp_ref, pieces_ref, part_ref, outer_part_ref, work, faces,
 ):
-    lanes = v_ref.shape[3]
-    rows = v_ref.shape[2] // SUBS
-    along = float(4 * v_ref.shape[2] * v_ref.shape[2])
-    vertical = 256.0
+    _, _, nx, lanes = down_ref.shape
+    rows = nx // SUBS
+    scale = float(2 * nx * nx)
     lane = lane_index((SUBS, lanes))
+    even = lax.axis_index("gy") % 2 == 0
+    for at in (pl.ds(i, SUBS) for i in range(0, nx, SUBS)):
+        own, chip, link = edge_ref[at], chip_ref[at], link_ref[at]
+        right, left = jnp.where(even, chip, link), jnp.where(even, link, chip)
+        right = pltpu.roll(right, lanes - 8, 1)
+        own_first = pltpu.roll(own, lanes - 8, 1)
+        upper = pltpu.roll(own + right, lanes - 4, 1) * (right - own)
+        lower = pltpu.roll(own_first + left, lanes - 4, 1) * (left - own_first)
+        faces[0, at] = scale * upper
+        faces[1, at] = scale * lower
 
     def load(c, k):
         f, z = divmod(c, 2)
         at = pl.ds(k, SUBS, stride=rows)
-        v, kap = v_ref[f, z, at], k_ref[f, z, at]
-        left, right = left_ref[at], right_ref[at]
-        v_next = jnp.where(lane == lanes - 1, pltpu.roll(right, lanes - 9 - c, 1), pltpu.roll(v, lanes - 1, 1))
-        k_next = jnp.where(lane == lanes - 1, pltpu.roll(right, lanes - 13 - c, 1), pltpu.roll(kap, lanes - 1, 1))
-        upper = (0.5 * along) * (kap + k_next) * (v_next - v)
-        v_left = pltpu.roll(left, (lanes - c) % lanes, 1)
-        k_left = pltpu.roll(left, lanes - 4 - c, 1)
-        first = (0.5 * along) * (kap + k_left) * (v - v_left)
-        lower = jnp.where(lane == 0, first, pltpu.roll(upper, 1, 1))
-        if z == 0:
-            v_up, k_up = v_ref[f, 1, at], k_ref[f, 1, at]
-            v_dn, k_dn = below_ref[0, f, at], below_ref[1, f, at]
-        else:
-            v_up, k_up = above_ref[0, f, at], above_ref[1, f, at]
-            v_dn, k_dn = v_ref[f, 0, at], k_ref[f, 0, at]
-        layers = (0.5 * vertical) * ((kap + k_up) * (v_up - v) - (kap + k_dn) * (v - v_dn))
-        return (upper - lower) + layers + (2.0 * v + s_ref[f, z, at])
+        own, other = (up_ref, above_ref) if z else (down_ref, below_ref)
+        v, kap = own[0, f, at], own[1, f, at]
+        beyond = (0.5 * VERTICAL) * (kap + other[1, f, at]) * (other[0, f, at] - v)
+        upper = pltpu.roll(faces[0, at], lanes - 1 - c, 1)
+        lower = pltpu.roll(faces[1, at], (lanes - c) % lanes, 1)
+        side = jnp.where(lane == lanes - 1, upper, jnp.where(lane == 0, lower, 0.0))
+        return local_ref[c, k] + beyond + side
 
     head, tail = reduce_sources(load, 4, rows, xi_ref, xo_ref, part_ref, outer_part_ref, work)
     send(pieces_ref, xp_ref, head, tail)
 
 
 def middle_kernel(
-    me_ref, pieces_ref, v_ref, xi_ref, xo_ref, part_ref, outer_part_ref, yi_ref, yo_ref, yp_ref,
+    pieces_ref, down_ref, up_ref, xi_ref, xo_ref, part_ref, outer_part_ref, yi_ref, yo_ref, yp_ref,
     out_pieces_ref, y_part_ref, y_outer_part_ref, work, swept, turned,
 ):
-    scale = float(2 * v_ref.shape[2] * v_ref.shape[2])
-    rows_x = v_ref.shape[2] // SUBS
-    rows_y = v_ref.shape[3] // SUBS
-    x_first, x_last = ends(pieces_ref, me_ref[0], scale)
+    _, _, nx, ny = down_ref.shape
+    scale = float(2 * nx * nx)
+    rows_x = nx // SUBS
+    rows_y = ny // SUBS
+    x_first, x_last = ends(pieces_ref, lax.axis_index("gx"), scale)
 
     def store(c, k, values):
         f, z = divmod(c, 2)
         at = pl.ds(k, SUBS, stride=rows_x)
-        swept[f, pl.ds(z * v_ref.shape[2] + k, SUBS, stride=rows_x)] = values - 2.0 * v_ref[f, z, at]
+        v = (up_ref if z else down_ref)[0, f, at]
+        swept[f, pl.ds(z * nx + k, SUBS, stride=rows_x)] = values - 2.0 * v
 
     expand(x_first, x_last, 4, rows_x, xi_ref, xo_ref, part_ref, outer_part_ref, work, store)
     for f in range(2):
@@ -252,29 +277,31 @@
     send(out_pieces_ref, yp_ref, head, tail)
 
 
-def last_kernel(me_ref, pieces_ref, v_ref, yi_ref, yo_ref, part_ref, outer_part_ref, out_ref, work, turned):
-    scale = float(2 * v_ref.shape[2] * v_ref.shape[2])
-    rows_y = v_ref.shape[3] // SUBS
-    x_first, x_last = ends(pieces_ref, me_ref[0], scale)
+def last_kernel(pieces_ref, down_ref, up_ref, yi_ref, yo_ref, part_ref, outer_part_ref, out_ref, work, turned):
+    _, _, nx, ny = down_ref.shape
+    scale = float(2 * nx * nx)
+    rows_y = ny // SUBS
+    x_first, x_last = ends(pieces_ref, lax.axis_index("gy"), scale)
 
     def store(c, k, values):
         turned[c, pl.ds(k, SUBS, stride=rows_y)] = values
 
     expand(x_first, x_last, 2, rows_y, yi_ref, yo_ref, part_ref, outer_part_ref, work, store)
     for f in range(2):
-        out_ref[f] = v_ref[f] + turned[f].T.reshape(v_ref.shape[1:])
-
-
-def call(kernel, outs, scratch, *args, scalars=0):
-    smem = pl.BlockSpec(memory_space=pltpu.SMEM)
+        both = turned[f].T
+        out_ref[f, 0] = down_ref[0, f] + both[:nx]
+        out_ref[f, 1] = up_ref[0, f] + both[nx:]
+
+
+def call(kernel, outs, scratch, *args, space=pltpu.VMEM, room=24):
     vmem = pl.BlockSpec(memory_space=pltpu.VMEM)
     return pl.pallas_call(
         kernel,
         out_shape=outs,
-        in_specs=[smem] * scalars + [vmem] * (len(args) - scalars),
+        in_specs=[pl.BlockSpec(memory_space=space)] * len(args),
         out_specs=[vmem] * len(outs),
-        scratch_shapes=[pltpu.VMEM(shape, F32) for shape in scratch],
-        compiler_params=pltpu.CompilerParams(vmem_limit_bytes=24 * 1024 * 1024),
+        scratch_shapes=scratch,
+        compiler_params=pltpu.CompilerParams(vmem_limit_bytes=room * 1024 * 1024),
     )(*args)
 
 
@@ -285,49 +312,53 @@
     )
 
 
+def swap(values, axis, start):
+    pairs = [(i, i + 1) for i in range(start, lax.axis_size(axis) - 1, 2)]
+    return lax.ppermute(values, axis, pairs + [(j, i) for i, j in pairs])
+
+
 def on_device(v, kappa, source):
     _, _, nx, ny = v.shape
     rows_x, rows_y = nx // SUBS, ny // SUBS
     gx, gy = lax.axis_size("gx"), lax.axis_size("gy")
+    layer = struct(2, 2, nx, ny)
     up, down, edge = call(
-        pack_kernel, [struct(2, 2, nx, ny), struct(2, 2, nx, ny), struct(nx, ny)], [], v, kappa
-    )
-    left = shift(edge, "gy", 1)
-    right = shift(edge, "gy", -1)
+        pack_kernel, [layer, layer, struct(nx, ny)], [pltpu.SemaphoreType.DMA((2, 2))],
+        pltpu.with_memory_space_constraint(v, pltpu.HBM), pltpu.with_memory_space_constraint(kappa, pltpu.HBM), space=pltpu.HBM, room=24,
+    )
     below = shift(up, "gz", 1)
     above = shift(down, "gz", -1)
-    xi, xo, xp, yi, yo, yp = call(
-        matrix_kernel,
+    chip = swap(edge, "gy", 0)
+    link = swap(edge, "gy", 1)
+    work = pltpu.VMEM((3, 4 * SUBS, ny), F32)
+    square = pltpu.VMEM((2, ny, 2 * nx), F32)
+    xi, xo, xp, yi, yo, yp, local = call(
+        local_kernel,
         [
             struct(3, 4, rows_x - 1, SUBS, ny), struct(3, SUBS - 1, 4, ny), struct(5, 4, ny),
-            struct(3, 2, rows_y - 1, SUBS, 128), struct(3, SUBS - 1, 2, 128), struct(5, 2, 128),
+            struct(3, 2, rows_y - 1, SUBS, 2 * nx), struct(3, SUBS - 1, 2, 2 * nx), struct(5, 2, 2 * nx),
+            struct(4, rows_x, SUBS, ny),
         ],
-        [(3, 4 * SUBS, 128), (2, 128, 128)],
-        kappa,
+        [work, square],
+        down, up, source,
     )
     pieces, x_part, x_outer = call(
         source_kernel,
         [struct(gx, 7, 4, ny), struct(4, rows_x - 1, SUBS, ny), struct(SUBS - 1, 4, ny)],
-        [(2, 4 * SUBS, 128)],
-        v, kappa, source, below, above, left, right, xi, xo, xp,
+        [work, pltpu.VMEM((2, nx, ny), F32)],
+        down, up, local, below, above, edge, chip, link, xi, xo, xp,
     )
     pieces = lax.all_to_all(pieces, "gx", 0, 0)
-    me = lax.axis_index("gx").astype(jnp.int32).reshape(1)
     pieces, y_part, y_outer = call(
         middle_kernel,
-        [struct(gy, 7, 2, 128), struct(2, rows_y - 1, SUBS, 128), struct(SUBS - 1, 2, 128)],
-        [(2, 4 * SUBS, 128), (2, 128, 128), (2, 128, 128)],
-        me, pieces, v, xi, xo, x_part, x_outer, yi, yo, yp,
-        scalars=1,
+        [struct(gy, 7, 2, 2 * nx), struct(2, rows_y - 1, SUBS, 2 * nx), struct(SUBS - 1, 2, 2 * nx)],
+        [work, square, square],
+        pieces, down, up, xi, xo, x_part, x_outer, yi, yo, yp,
     )
     pieces = lax.all_to_all(pieces, "gy", 0, 0)
-    me = lax.axis_index("gy").astype(jnp.int32).reshape(1)
     (out,) = call(
-        last_kernel,
-        [struct(*v.shape)],
-        [(2, 4 * SUBS, 128), (2, 128, 128)],
-        me, pieces, v, yi, yo, y_part, y_outer,
-        scalars=1,
+        last_kernel, [struct(*v.shape)], [work, square],
+        pieces, down, up, yi, yo, y_part, y_outer,
     )
     return out
 

time: 62 us -> 57.8 us (0.932)
  the two profiles are of different devices: /device:TPU:56 before, /device:TPU:1 now
where the time goes in v2:
time: 57.8 us; the launch traced here: 57.5 us
  blocking collectives  38.3 us (66%)
  starting transfers between devices  15.3 us (26%)
  Pallas kernels  3.39 us (6%)
    all_to_all x1, blocking collectives, on_device(): pieces = lax.all_to_all(pieces, 'gx', 0, 0)  25.6 us
    all_to_all x1, blocking collectives, on_device(): pieces = lax.all_to_all(pieces, 'gy', 0, 0)  12.7 us
    ppermute x2, starting transfers between devices, swap(): return lax.ppermute(values, axis, pairs + [(j, i) for i, j in pairs])  9.34 us
    ppermute x2, starting transfers between devices, shift(): lax.ppermute(values, axis, [(i, i + step) for i in range(peers) if 0 <= i...  5.96 us
    pallas_call x5, Pallas kernels, call(): pl.pallas_call(kernel, out_shape=outs, in_specs=[pl.BlockSpec(memory_spac...  3.39 us
  transfers between devices with their start and end apart: 4, of which 1 were waited for; matrix products, arithmetic and copies ran while one was open for 0% of the time, Pallas kernels for 1%

profile of v2, /device:TPU:1, one launch (start us, length us, event | category | flops | bytes accessed | tf_op | source)
XLA Modules:
  0.0 57.5 jit_solution(16307945376431466997)
XLA Ops:
  0.0 0.0 copy-start
  0.0 1.2 %shard_map.37 = (f32[2,2,64,128]{3,2,1,0:T(8,128)S(1)}, f32[2,2,64,128]{3,2,1,0:T(8,128)S(1)}, f32[64,128]{1,0:T(8,128)S(1)}) custom-call(f32[2,2,64,128]{3,2,1,0:T(8,128)} %v_hbm.1, f32[2,2,64,128]{3,2,1,0:T(8,128)} %k_hbm.1), custom_call_target="tpu_custom_call" | custom-call | tf_op jit(solution)/shard_map/pallas_call | solution.py:298
  1.2 1.3 %collective-permute-start.1 = (f32[2,2,64,128]{3,2,1,0:T(8,128)S(1)}, f32[2,2,64,128]{3,2,1,0:T(8,128)S(1)}, u32[]{:S(2)}, u32[]{:S(2)}) collective-permute-start(f32[2,2,64,128]{3,2,1,0:T(8,128)S(1)} %get-tuple-element.21.down_ref), channel_id=1, source_target_pairs={{1,0},{2,1},{3,2},{5,4},{6,5},{7,6},{9,8},{10,9},{11,10},{13,12},{... | collective-permute-start | bytes 393224 | tf_op jit(solution)/shard_map/ppermute | solution.py:310
  2.5 4.7 %collective-permute-start = (f32[2,2,64,128]{3,2,1,0:T(8,128)S(1)}, f32[2,2,64,128]{3,2,1,0:T(8,128)S(1)}, u32[]{:S(2)}, u32[]{:S(2)}) collective-permute-start(f32[2,2,64,128]{3,2,1,0:T(8,128)S(1)} %get-tuple-element.22.up_ref), channel_id=1, source_target_pairs={{0,1},{1,2},{2,3},{4,5},{5,6},{6,7},{8,9},{9,10},{10,11},{12,13},{... | collective-permute-start | bytes 393224 | tf_op jit(solution)/shard_map/ppermute | solution.py:310
  7.2 4.4 %collective-permute-start.3 = (f32[64,128]{1,0:T(8,128)S(1)}, f32[64,128]{1,0:T(8,128)S(1)}, u32[]{:S(2)}, u32[]{:S(2)}) collective-permute-start(f32[64,128]{1,0:T(8,128)S(1)} %get-tuple-element.24.edge_ref), channel_id=1, source_target_pairs={{4,8},{12,16},{20,24},{8,4},{16,12},{24,20},{5,9},{13,17},{21,25},... | collective-permute-start | bytes 98312 | tf_op jit(solution)/shard_map/ppermute | solution.py:317
  11.6 4.9 %collective-permute-start.2 = (f32[64,128]{1,0:T(8,128)S(1)}, f32[64,128]{1,0:T(8,128)S(1)}, u32[]{:S(2)}, u32[]{:S(2)}) collective-permute-start(f32[64,128]{1,0:T(8,128)S(1)} %get-tuple-element.24.edge_ref), channel_id=1, source_target_pairs={{0,4},{8,12},{16,20},{24,28},{4,0},{12,8},{20,16},{28,24},{1,5},{9... | collective-permute-start | bytes 98312 | tf_op jit(solution)/shard_map/ppermute | solution.py:317
  16.5 0.0 copy-done
  16.6 0.4 shard_map.38
  17.0 0.0 collective-permute-done.3.link_ref
  17.0 0.4 collective-permute-done.2.chip_ref
  17.4 0.0 collective-permute-done.1.above_ref
  17.4 0.0 collective-permute-done.below_ref
  17.4 0.4 shard_map.39
  17.8 25.6 %all_to_all.10.pieces_ref = f32[16,7,4,128]{3,2,1,0:T(4,128)S(1)} all-to-all(f32[16,7,4,128]{3,2,1,0:T(4,128)S(1)} %get-tuple-element.28), channel_id=1, replica_groups=mesh['gx'=16,'gy'=8,'gz'=4] {'gx'}, dimensions={0} | all-to-all | bytes 458752 | tf_op jit(solution)/shard_map/all_to_all | solution.py:351
  43.3 0.5 shard_map.40
  43.8 12.7 %all_to_all.11.pieces_ref = f32[8,7,2,128]{3,2,1,0:T(2,128)S(1)} all-to-all(f32[8,7,2,128]{3,2,1,0:T(2,128)S(1)} %get-tuple-element.34), channel_id=1, replica_groups=mesh['gx'=16,'gy'=8,'gz'=4] {'gy'}, dimensions={0} | all-to-all | bytes 114688 | tf_op jit(solution)/shard_map/all_to_all | solution.py:358
  56.6 0.9 %shard_map.41 = f32[2,2,64,128]{3,2,1,0:T(8,128)} custom-call(f32[8,7,2,128]{3,2,1,0:T(2,128)S(1)} %all_to_all.11.pieces_ref, f32[2,2,64,128]{3,2,1,0:T(8,128)S(1)} %get-tuple-element.21.down_ref, f32[2,2,64,128]{3,2,1,0:T(8,128)S(1)} %get-tuple-element.22.up_ref, f32[3,2,15,8,128]{4,3,2,1,0:T(8,128)S(1)} %get-tuple-element.31.yi_ref, ...), custom_call_target="tpu_custom_call" | custom-call | tf_op jit(solution)/shard_map/pallas_call | solution.py:298
Async XLA Ops:
  0.0 16.5 %copy-start = (f32[2,2,64,128]{3,2,1,0:T(8,128)S(1)}, f32[2,2,64,128]{3,2,1,0:T(8,128)}, u32[]{:S(2)}) copy-start(f32[2,2,64,128]{3,2,1,0:T(8,128)} %s_ref.1) | copy-start | bytes 393220
  1.2 16.2 %collective-permute-start.1 = (f32[2,2,64,128]{3,2,1,0:T(8,128)S(1)}, f32[2,2,64,128]{3,2,1,0:T(8,128)S(1)}, u32[]{:S(2)}, u32[]{:S(2)}) collective-permute-start(f32[2,2,64,128]{3,2,1,0:T(8,128)S(1)} %get-tuple-element.21.down_ref), channel_id=1, source_target_pairs={{1,0},{2,1},{3,2},{5,4},{6,5},{7,6},{9,8},{10,9},{11,10},{13,12},{... | collective-permute-start | bytes 393224 | tf_op jit(solution)/shard_map/ppermute | solution.py:310
  2.5 14.9 %collective-permute-start = (f32[2,2,64,128]{3,2,1,0:T(8,128)S(1)}, f32[2,2,64,128]{3,2,1,0:T(8,128)S(1)}, u32[]{:S(2)}, u32[]{:S(2)}) collective-permute-start(f32[2,2,64,128]{3,2,1,0:T(8,128)S(1)} %get-tuple-element.22.up_ref), channel_id=1, source_target_pairs={{0,1},{1,2},{2,3},{4,5},{5,6},{6,7},{8,9},{9,10},{10,11},{12,13},{... | collective-permute-start | bytes 393224 | tf_op jit(solution)/shard_map/ppermute | solution.py:310
  7.2 9.8 %collective-permute-start.3 = (f32[64,128]{1,0:T(8,128)S(1)}, f32[64,128]{1,0:T(8,128)S(1)}, u32[]{:S(2)}, u32[]{:S(2)}) collective-permute-start(f32[64,128]{1,0:T(8,128)S(1)} %get-tuple-element.24.edge_ref), channel_id=1, source_target_pairs={{4,8},{12,16},{20,24},{8,4},{16,12},{24,20},{5,9},{13,17},{21,25},... | collective-permute-start | bytes 98312 | tf_op jit(solution)/shard_map/ppermute | solution.py:317
  11.6 5.8 %collective-permute-start.2 = (f32[64,128]{1,0:T(8,128)S(1)}, f32[64,128]{1,0:T(8,128)S(1)}, u32[]{:S(2)}, u32[]{:S(2)}) collective-permute-start(f32[64,128]{1,0:T(8,128)S(1)} %get-tuple-element.24.edge_ref), channel_id=1, source_target_pairs={{0,4},{8,12},{16,20},{24,28},{4,0},{12,8},{20,16},{28,24},{1,5},{9... | collective-permute-start | bytes 98312 | tf_op jit(solution)/shard_map/ppermute | solution.py:317

commit v3 on v2

--- a/solution.py
+++ b/solution.py
@@ -157,11 +157,19 @@
         pieces_ref[d, 6] = tail
 
 
-def ends(pieces_ref, me, scale):
+def order(axis):
+    return {"gx": [8, 0, 15, 1, 14, 2, 13, 3, 12, 4, 11, 5, 10, 6, 9, 7], "gy": [5, 4, 6, 7, 0, 1, 2, 3]}[axis]
+
+
+def ends(pieces_ref, me, scale, order):
     blocks = pieces_ref.shape[0]
+    mine = sum(jnp.where(me == j, i, 0) for i, j in enumerate(order))
+
+    def at(j):
+        return mine if j is me else order.index(j)
 
     def piece(j):
-        return [pieces_ref[j, q] for q in range(7)]
+        return [pieces_ref[at(j), q] for q in range(7)]
 
     half = 0.5 * scale
 
@@ -172,27 +180,27 @@
         q = face / (total + face * xt)
         return total * q, q * (xt * far_src + t * (source + near_src))
 
-    left_leak = half * pieces_ref[0, 3]
+    left_leak = half * pieces_ref[at(0), 3]
     left_src = jnp.zeros_like(left_leak)
-    right_leak = half * pieces_ref[blocks - 1, 4]
+    right_leak = half * pieces_ref[at(blocks - 1), 4]
     right_src = jnp.zeros_like(right_leak)
     for step in range(blocks - 1):
         a, t, b, k_first, k_last, r_first, r_last = piece(step)
-        face = half * (k_last + pieces_ref[step + 1, 3])
+        face = half * (k_last + pieces_ref[at(step + 1), 3])
         leak, src = through(left_leak, left_src, a, t, b, r_first, r_last, face)
         left_leak = jnp.where(step < me, leak, left_leak)
         left_src = jnp.where(step < me, src, left_src)
         j = blocks - 1 - step
         a, t, b, k_first, k_last, r_first, r_last = piece(j)
-        face = half * (k_first + pieces_ref[j - 1, 4])
+        face = half * (k_first + pieces_ref[at(j - 1), 4])
         leak, src = through(right_leak, right_src, b, t, a, r_last, r_first, face)
         right_leak = jnp.where(j > me, leak, right_leak)
         right_src = jnp.where(j > me, src, right_src)
-    a, t, b = (pieces_ref[me, q] for q in range(3))
+    a, t, b = (pieces_ref[at(me), q] for q in range(3))
     first = a + left_leak
     last = b + right_leak
-    r_first = pieces_ref[me, 5] + left_src
-    r_last = pieces_ref[me, 6] + right_src
+    r_first = pieces_ref[at(me), 5] + left_src
+    r_last = pieces_ref[at(me), 6] + right_src
     inv = 1.0 / (first * last + t * (first + last))
     return inv * ((last + t) * r_first + t * r_last), inv * (t * r_first + (first + t) * r_last)
 
@@ -259,7 +267,7 @@
     scale = float(2 * nx * nx)
     rows_x = nx // SUBS
     rows_y = ny // SUBS
-    x_first, x_last = ends(pieces_ref, lax.axis_index("gx"), scale)
+    x_first, x_last = ends(pieces_ref, lax.axis_index("gx"), scale, order("gx"))
 
     def store(c, k, values):
         f, z = divmod(c, 2)
@@ -281,7 +289,7 @@
     _, _, nx, ny = down_ref.shape
     scale = float(2 * nx * nx)
     rows_y = ny // SUBS
-    x_first, x_last = ends(pieces_ref, lax.axis_index("gy"), scale)
+    x_first, x_last = ends(pieces_ref, lax.axis_index("gy"), scale, order("gy"))
 
     def store(c, k, values):
         turned[c, pl.ds(k, SUBS, stride=rows_y)] = values
@@ -310,6 +318,10 @@
     return lax.ppermute(
         values, axis, [(i, i + step) for i in range(peers) if 0 <= i + step < peers]
     )
+
+
+def exchange(pieces, axis):
+    return lax.all_to_all(pieces, axis, 0, 0, axis_index_groups=[order(axis)])
 
 
 def swap(values, axis, start):
@@ -348,14 +360,14 @@
         [work, pltpu.VMEM((2, nx, ny), F32)],
         down, up, local, below, above, edge, chip, link, xi, xo, xp,
     )
-    pieces = lax.all_to_all(pieces, "gx", 0, 0)
+    pieces = exchange(pieces, "gx")
     pieces, y_part, y_outer = call(
         middle_kernel,
         [struct(gy, 7, 2, 2 * nx), struct(2, rows_y - 1, SUBS, 2 * nx), struct(SUBS - 1, 2, 2 * nx)],
         [work, square, square],
         pieces, down, up, xi, xo, x_part, x_outer, yi, yo, yp,
     )
-    pieces = lax.all_to_all(pieces, "gy", 0, 0)
+    pieces = exchange(pieces, "gy")
     (out,) = call(
         last_kernel, [struct(*v.shape)], [work, square],
         pieces, down, up, yi, yo, y_part, y_outer,

time: 57.8 us -> 52.8 us (0.913)
  blocking collectives: 38.3 us -> 33.4 us
    all_to_all x2, blocking collectives: 38.3 us -> 33.4 us  [exchange(): return lax.all_to_all(pieces, axis, 0, 0, axis_index_groups=[order(axis)])]
where the time goes in v3:
time: 52.8 us; the launch traced here: 52.5 us
  blocking collectives  33.4 us (63%)
  starting transfers between devices  15.3 us (29%)
  Pallas kernels  3.38 us (6%)
    all_to_all x2, blocking collectives, exchange(): return lax.all_to_all(pieces, axis, 0, 0, axis_index_groups=[order(axis)])  33.4 us
    ppermute x2, starting transfers between devices, swap(): return lax.ppermute(values, axis, pairs + [(j, i) for i, j in pairs])  9.34 us
    ppermute x2, starting transfers between devices, shift(): lax.ppermute(values, axis, [(i, i + step) for i in range(peers) if 0 <= i...  5.96 us
    pallas_call x5, Pallas kernels, call(): pl.pallas_call(kernel, out_shape=outs, in_specs=[pl.BlockSpec(memory_spac...  3.38 us
  transfers between devices with their start and end apart: 4, of which 1 were waited for; matrix products, arithmetic and copies ran while one was open for 0% of the time, Pallas kernels for 1%

profile of v3, /device:TPU:1, one launch (start us, length us, event | category | flops | bytes accessed | tf_op | source)
XLA Modules:
  0.0 52.5 jit_solution(9526670919364622924)
XLA Ops:
  0.0 0.0 copy-start
  0.0 1.2 %shard_map.37 = (f32[2,2,64,128]{3,2,1,0:T(8,128)S(1)}, f32[2,2,64,128]{3,2,1,0:T(8,128)S(1)}, f32[64,128]{1,0:T(8,128)S(1)}) custom-call(f32[2,2,64,128]{3,2,1,0:T(8,128)} %v_hbm.1, f32[2,2,64,128]{3,2,1,0:T(8,128)} %k_hbm.1), custom_call_target="tpu_custom_call" | custom-call | tf_op jit(solution)/shard_map/pallas_call | solution.py:306
  1.2 1.3 %collective-permute-start.1 = (f32[2,2,64,128]{3,2,1,0:T(8,128)S(1)}, f32[2,2,64,128]{3,2,1,0:T(8,128)S(1)}, u32[]{:S(2)}, u32[]{:S(2)}) collective-permute-start(f32[2,2,64,128]{3,2,1,0:T(8,128)S(1)} %get-tuple-element.21.down_ref), channel_id=1, source_target_pairs={{1,0},{2,1},{3,2},{5,4},{6,5},{7,6},{9,8},{10,9},{11,10},{13,12},{... | collective-permute-start | bytes 393224 | tf_op jit(solution)/shard_map/ppermute | solution.py:318
  2.5 4.7 %collective-permute-start = (f32[2,2,64,128]{3,2,1,0:T(8,128)S(1)}, f32[2,2,64,128]{3,2,1,0:T(8,128)S(1)}, u32[]{:S(2)}, u32[]{:S(2)}) collective-permute-start(f32[2,2,64,128]{3,2,1,0:T(8,128)S(1)} %get-tuple-element.22.up_ref), channel_id=1, source_target_pairs={{0,1},{1,2},{2,3},{4,5},{5,6},{6,7},{8,9},{9,10},{10,11},{12,13},{... | collective-permute-start | bytes 393224 | tf_op jit(solution)/shard_map/ppermute | solution.py:318
  7.2 4.4 %collective-permute-start.3 = (f32[64,128]{1,0:T(8,128)S(1)}, f32[64,128]{1,0:T(8,128)S(1)}, u32[]{:S(2)}, u32[]{:S(2)}) collective-permute-start(f32[64,128]{1,0:T(8,128)S(1)} %get-tuple-element.24.edge_ref), channel_id=1, source_target_pairs={{4,8},{12,16},{20,24},{8,4},{16,12},{24,20},{5,9},{13,17},{21,25},... | collective-permute-start | bytes 98312 | tf_op jit(solution)/shard_map/ppermute | solution.py:329
  11.6 4.9 %collective-permute-start.2 = (f32[64,128]{1,0:T(8,128)S(1)}, f32[64,128]{1,0:T(8,128)S(1)}, u32[]{:S(2)}, u32[]{:S(2)}) collective-permute-start(f32[64,128]{1,0:T(8,128)S(1)} %get-tuple-element.24.edge_ref), channel_id=1, source_target_pairs={{0,4},{8,12},{16,20},{24,28},{4,0},{12,8},{20,16},{28,24},{1,5},{9... | collective-permute-start | bytes 98312 | tf_op jit(solution)/shard_map/ppermute | solution.py:329
  16.5 0.0 copy-done
  16.6 0.4 shard_map.38
  17.0 0.0 collective-permute-done.3.link_ref
  17.0 0.4 collective-permute-done.2.chip_ref
  17.4 0.0 collective-permute-done.1.above_ref
  17.4 0.0 collective-permute-done.below_ref
  17.4 0.4 shard_map.39
  17.8 26.0 %all_to_all.10.pieces_ref = f32[16,7,4,128]{3,2,1,0:T(4,128)S(1)} all-to-all(f32[16,7,4,128]{3,2,1,0:T(4,128)S(1)} %get-tuple-element.28), channel_id=1, replica_groups={{256,0,480,32,448,64,416,96,384,128,352,160,320,192,288,224},{257,1,481..., dimensions={0} | all-to-all | bytes 458752 | tf_op jit(solution)/shard_map/all_to_all | solution.py:324
  43.8 0.5 shard_map.40
  44.3 7.3 %all_to_all.11.pieces_ref = f32[8,7,2,128]{3,2,1,0:T(2,128)S(1)} all-to-all(f32[8,7,2,128]{3,2,1,0:T(2,128)S(1)} %get-tuple-element.34), channel_id=1, replica_groups={{20,16,24,28,0,4,8,12},{21,17,25,29,1,5,9,13},{22,18,26,30,2,6,10,14},{..., dimensions={0} | all-to-all | bytes 114688 | tf_op jit(solution)/shard_map/all_to_all | solution.py:324
  51.6 0.9 %shard_map.41 = f32[2,2,64,128]{3,2,1,0:T(8,128)} custom-call(f32[8,7,2,128]{3,2,1,0:T(2,128)S(1)} %all_to_all.11.pieces_ref, f32[2,2,64,128]{3,2,1,0:T(8,128)S(1)} %get-tuple-element.21.down_ref, f32[2,2,64,128]{3,2,1,0:T(8,128)S(1)} %get-tuple-element.22.up_ref, f32[3,2,15,8,128]{4,3,2,1,0:T(8,128)S(1)} %get-tuple-element.31.yi_ref, ...), custom_call_target="tpu_custom_call" | custom-call | tf_op jit(solution)/shard_map/pallas_call | solution.py:306
Async XLA Ops:
  0.0 16.5 %copy-start = (f32[2,2,64,128]{3,2,1,0:T(8,128)S(1)}, f32[2,2,64,128]{3,2,1,0:T(8,128)}, u32[]{:S(2)}) copy-start(f32[2,2,64,128]{3,2,1,0:T(8,128)} %s_ref.1) | copy-start | bytes 393220
  1.2 16.2 %collective-permute-start.1 = (f32[2,2,64,128]{3,2,1,0:T(8,128)S(1)}, f32[2,2,64,128]{3,2,1,0:T(8,128)S(1)}, u32[]{:S(2)}, u32[]{:S(2)}) collective-permute-start(f32[2,2,64,128]{3,2,1,0:T(8,128)S(1)} %get-tuple-element.21.down_ref), channel_id=1, source_target_pairs={{1,0},{2,1},{3,2},{5,4},{6,5},{7,6},{9,8},{10,9},{11,10},{13,12},{... | collective-permute-start | bytes 393224 | tf_op jit(solution)/shard_map/ppermute | solution.py:318
  2.5 14.9 %collective-permute-start = (f32[2,2,64,128]{3,2,1,0:T(8,128)S(1)}, f32[2,2,64,128]{3,2,1,0:T(8,128)S(1)}, u32[]{:S(2)}, u32[]{:S(2)}) collective-permute-start(f32[2,2,64,128]{3,2,1,0:T(8,128)S(1)} %get-tuple-element.22.up_ref), channel_id=1, source_target_pairs={{0,1},{1,2},{2,3},{4,5},{5,6},{6,7},{8,9},{9,10},{10,11},{12,13},{... | collective-permute-start | bytes 393224 | tf_op jit(solution)/shard_map/ppermute | solution.py:318
  7.2 9.8 %collective-permute-start.3 = (f32[64,128]{1,0:T(8,128)S(1)}, f32[64,128]{1,0:T(8,128)S(1)}, u32[]{:S(2)}, u32[]{:S(2)}) collective-permute-start(f32[64,128]{1,0:T(8,128)S(1)} %get-tuple-element.24.edge_ref), channel_id=1, source_target_pairs={{4,8},{12,16},{20,24},{8,4},{16,12},{24,20},{5,9},{13,17},{21,25},... | collective-permute-start | bytes 98312 | tf_op jit(solution)/shard_map/ppermute | solution.py:329
  11.6 5.8 %collective-permute-start.2 = (f32[64,128]{1,0:T(8,128)S(1)}, f32[64,128]{1,0:T(8,128)S(1)}, u32[]{:S(2)}, u32[]{:S(2)}) collective-permute-start(f32[64,128]{1,0:T(8,128)S(1)} %get-tuple-element.24.edge_ref), channel_id=1, source_target_pairs={{0,4},{8,12},{16,20},{24,28},{4,0},{12,8},{20,16},{28,24},{1,5},{9... | collective-permute-start | bytes 98312 | tf_op jit(solution)/shard_map/ppermute | solution.py:329

commit v4 on v3

--- a/solution.py
+++ b/solution.py
@@ -158,7 +158,7 @@
 
 
 def order(axis):
-    return {"gx": [8, 0, 15, 1, 14, 2, 13, 3, 12, 4, 11, 5, 10, 6, 9, 7], "gy": [5, 4, 6, 7, 0, 1, 2, 3]}[axis]
+    return {"gx": [10, 1, 0, 2, 3, 15, 14, 13, 4, 12, 5, 11, 6, 9, 7, 8], "gy": [5, 4, 0, 1, 2, 3, 7, 6]}[axis]
 
 
 def ends(pieces_ref, me, scale, order):
@@ -301,7 +301,7 @@
         out_ref[f, 1] = up_ref[0, f] + both[nx:]
 
 
-def call(kernel, outs, scratch, *args, space=pltpu.VMEM, room=24):
+def call(kernel, outs, scratch, *args, space=pltpu.VMEM):
     vmem = pl.BlockSpec(memory_space=pltpu.VMEM)
     return pl.pallas_call(
         kernel,
@@ -309,7 +309,7 @@
         in_specs=[pl.BlockSpec(memory_space=space)] * len(args),
         out_specs=[vmem] * len(outs),
         scratch_shapes=scratch,
-        compiler_params=pltpu.CompilerParams(vmem_limit_bytes=room * 1024 * 1024),
+        compiler_params=pltpu.CompilerParams(vmem_limit_bytes=24 * 1024 * 1024),
     )(*args)
 
 
@@ -336,7 +336,7 @@
     layer = struct(2, 2, nx, ny)
     up, down, edge = call(
         pack_kernel, [layer, layer, struct(nx, ny)], [pltpu.SemaphoreType.DMA((2, 2))],
-        pltpu.with_memory_space_constraint(v, pltpu.HBM), pltpu.with_memory_space_constraint(kappa, pltpu.HBM), space=pltpu.HBM, room=24,
+        pltpu.with_memory_space_constraint(v, pltpu.HBM), pltpu.with_memory_space_constraint(kappa, pltpu.HBM), space=pltpu.HBM,
     )
     below = shift(up, "gz", 1)
     above = shift(down, "gz", -1)

time: 52.8 us -> 51.7 us (0.979)
  blocking collectives: 33.4 us -> 32.3 us
    all_to_all x2, blocking collectives: 33.4 us -> 32.3 us  [exchange(): return lax.all_to_all(pieces, axis, 0, 0, axis_index_groups=[order(axis)])]
where the time goes in v4:
time: 51.7 us; the launch traced here: 51.4 us
  blocking collectives  32.3 us (62%)
  starting transfers between devices  15.3 us (30%)
  Pallas kernels  3.38 us (7%)
    all_to_all x2, blocking collectives, exchange(): return lax.all_to_all(pieces, axis, 0, 0, axis_index_groups=[order(axis)])  32.3 us
    ppermute x2, starting transfers between devices, swap(): return lax.ppermute(values, axis, pairs + [(j, i) for i, j in pairs])  9.34 us
    ppermute x2, starting transfers between devices, shift(): lax.ppermute(values, axis, [(i, i + step) for i in range(peers) if 0 <= i...  5.96 us
    pallas_call x5, Pallas kernels, call(): pl.pallas_call(kernel, out_shape=outs, in_specs=[pl.BlockSpec(memory_spac...  3.38 us
  transfers between devices with their start and end apart: 4, of which 1 were waited for; matrix products, arithmetic and copies ran while one was open for 0% of the time, Pallas kernels for 1%

profile of v4, /device:TPU:1, one launch (start us, length us, event | category | flops | bytes accessed | tf_op | source)
XLA Modules:
  0.0 51.4 jit_solution(17617836912755795548)
XLA Ops:
  0.0 0.0 copy-start
  0.0 1.2 %shard_map.37 = (f32[2,2,64,128]{3,2,1,0:T(8,128)S(1)}, f32[2,2,64,128]{3,2,1,0:T(8,128)S(1)}, f32[64,128]{1,0:T(8,128)S(1)}) custom-call(f32[2,2,64,128]{3,2,1,0:T(8,128)} %v_hbm.1, f32[2,2,64,128]{3,2,1,0:T(8,128)} %k_hbm.1), custom_call_target="tpu_custom_call" | custom-call | tf_op jit(solution)/shard_map/pallas_call | solution.py:306
  1.2 1.3 %collective-permute-start.1 = (f32[2,2,64,128]{3,2,1,0:T(8,128)S(1)}, f32[2,2,64,128]{3,2,1,0:T(8,128)S(1)}, u32[]{:S(2)}, u32[]{:S(2)}) collective-permute-start(f32[2,2,64,128]{3,2,1,0:T(8,128)S(1)} %get-tuple-element.21.down_ref), channel_id=1, source_target_pairs={{1,0},{2,1},{3,2},{5,4},{6,5},{7,6},{9,8},{10,9},{11,10},{13,12},{... | collective-permute-start | bytes 393224 | tf_op jit(solution)/shard_map/ppermute | solution.py:318
  2.5 4.7 %collective-permute-start = (f32[2,2,64,128]{3,2,1,0:T(8,128)S(1)}, f32[2,2,64,128]{3,2,1,0:T(8,128)S(1)}, u32[]{:S(2)}, u32[]{:S(2)}) collective-permute-start(f32[2,2,64,128]{3,2,1,0:T(8,128)S(1)} %get-tuple-element.22.up_ref), channel_id=1, source_target_pairs={{0,1},{1,2},{2,3},{4,5},{5,6},{6,7},{8,9},{9,10},{10,11},{12,13},{... | collective-permute-start | bytes 393224 | tf_op jit(solution)/shard_map/ppermute | solution.py:318
  7.2 4.4 %collective-permute-start.3 = (f32[64,128]{1,0:T(8,128)S(1)}, f32[64,128]{1,0:T(8,128)S(1)}, u32[]{:S(2)}, u32[]{:S(2)}) collective-permute-start(f32[64,128]{1,0:T(8,128)S(1)} %get-tuple-element.24.edge_ref), channel_id=1, source_target_pairs={{4,8},{12,16},{20,24},{8,4},{16,12},{24,20},{5,9},{13,17},{21,25},... | collective-permute-start | bytes 98312 | tf_op jit(solution)/shard_map/ppermute | solution.py:329
  11.6 4.9 %collective-permute-start.2 = (f32[64,128]{1,0:T(8,128)S(1)}, f32[64,128]{1,0:T(8,128)S(1)}, u32[]{:S(2)}, u32[]{:S(2)}) collective-permute-start(f32[64,128]{1,0:T(8,128)S(1)} %get-tuple-element.24.edge_ref), channel_id=1, source_target_pairs={{0,4},{8,12},{16,20},{24,28},{4,0},{12,8},{20,16},{28,24},{1,5},{9... | collective-permute-start | bytes 98312 | tf_op jit(solution)/shard_map/ppermute | solution.py:329
  16.5 0.0 copy-done
  16.6 0.4 shard_map.38
  17.0 0.0 collective-permute-done.3.link_ref
  17.0 0.4 collective-permute-done.2.chip_ref
  17.4 0.0 collective-permute-done.1.above_ref
  17.4 0.0 collective-permute-done.below_ref
  17.4 0.4 shard_map.39
  17.8 25.0 %all_to_all.10.pieces_ref = f32[16,7,4,128]{3,2,1,0:T(4,128)S(1)} all-to-all(f32[16,7,4,128]{3,2,1,0:T(4,128)S(1)} %get-tuple-element.28), channel_id=1, replica_groups={{320,32,0,64,96,480,448,416,128,384,160,352,192,288,224,256},{321,33,1,..., dimensions={0} | all-to-all | bytes 458752 | tf_op jit(solution)/shard_map/all_to_all | solution.py:324
  42.7 0.5 shard_map.40
  43.2 7.3 %all_to_all.11.pieces_ref = f32[8,7,2,128]{3,2,1,0:T(2,128)S(1)} all-to-all(f32[8,7,2,128]{3,2,1,0:T(2,128)S(1)} %get-tuple-element.34), channel_id=1, replica_groups={{20,16,0,4,8,12,28,24},{21,17,1,5,9,13,29,25},{22,18,2,6,10,14,30,26},{..., dimensions={0} | all-to-all | bytes 114688 | tf_op jit(solution)/shard_map/all_to_all | solution.py:324
  50.5 0.9 %shard_map.41 = f32[2,2,64,128]{3,2,1,0:T(8,128)} custom-call(f32[8,7,2,128]{3,2,1,0:T(2,128)S(1)} %all_to_all.11.pieces_ref, f32[2,2,64,128]{3,2,1,0:T(8,128)S(1)} %get-tuple-element.21.down_ref, f32[2,2,64,128]{3,2,1,0:T(8,128)S(1)} %get-tuple-element.22.up_ref, f32[3,2,15,8,128]{4,3,2,1,0:T(8,128)S(1)} %get-tuple-element.31.yi_ref, ...), custom_call_target="tpu_custom_call" | custom-call | tf_op jit(solution)/shard_map/pallas_call | solution.py:306
Async XLA Ops:
  0.0 16.5 %copy-start = (f32[2,2,64,128]{3,2,1,0:T(8,128)S(1)}, f32[2,2,64,128]{3,2,1,0:T(8,128)}, u32[]{:S(2)}) copy-start(f32[2,2,64,128]{3,2,1,0:T(8,128)} %s_ref.1) | copy-start | bytes 393220
  1.2 16.2 %collective-permute-start.1 = (f32[2,2,64,128]{3,2,1,0:T(8,128)S(1)}, f32[2,2,64,128]{3,2,1,0:T(8,128)S(1)}, u32[]{:S(2)}, u32[]{:S(2)}) collective-permute-start(f32[2,2,64,128]{3,2,1,0:T(8,128)S(1)} %get-tuple-element.21.down_ref), channel_id=1, source_target_pairs={{1,0},{2,1},{3,2},{5,4},{6,5},{7,6},{9,8},{10,9},{11,10},{13,12},{... | collective-permute-start | bytes 393224 | tf_op jit(solution)/shard_map/ppermute | solution.py:318
  2.5 14.9 %collective-permute-start = (f32[2,2,64,128]{3,2,1,0:T(8,128)S(1)}, f32[2,2,64,128]{3,2,1,0:T(8,128)S(1)}, u32[]{:S(2)}, u32[]{:S(2)}) collective-permute-start(f32[2,2,64,128]{3,2,1,0:T(8,128)S(1)} %get-tuple-element.22.up_ref), channel_id=1, source_target_pairs={{0,1},{1,2},{2,3},{4,5},{5,6},{6,7},{8,9},{9,10},{10,11},{12,13},{... | collective-permute-start | bytes 393224 | tf_op jit(solution)/shard_map/ppermute | solution.py:318
  7.2 9.8 %collective-permute-start.3 = (f32[64,128]{1,0:T(8,128)S(1)}, f32[64,128]{1,0:T(8,128)S(1)}, u32[]{:S(2)}, u32[]{:S(2)}) collective-permute-start(f32[64,128]{1,0:T(8,128)S(1)} %get-tuple-element.24.edge_ref), channel_id=1, source_target_pairs={{4,8},{12,16},{20,24},{8,4},{16,12},{24,20},{5,9},{13,17},{21,25},... | collective-permute-start | bytes 98312 | tf_op jit(solution)/shard_map/ppermute | solution.py:329
  11.6 5.8 %collective-permute-start.2 = (f32[64,128]{1,0:T(8,128)S(1)}, f32[64,128]{1,0:T(8,128)S(1)}, u32[]{:S(2)}, u32[]{:S(2)}) collective-permute-start(f32[64,128]{1,0:T(8,128)S(1)} %get-tuple-element.24.edge_ref), channel_id=1, source_target_pairs={{0,4},{8,12},{16,20},{24,28},{4,0},{12,8},{20,16},{28,24},{1,5},{9... | collective-permute-start | bytes 98312 | tf_op jit(solution)/shard_map/ppermute | solution.py:329

commit v5 on v4

--- a/solution.py
+++ b/solution.py
@@ -22,7 +22,7 @@
     return lax.broadcasted_iota(jnp.int32, shape, len(shape) - 2)
 
 
-def pack_kernel(v_hbm, k_hbm, up_ref, down_ref, edge_ref, sems):
+def pack_kernel(v_hbm, k_hbm, up_ref, down_ref, edge_ref, near_ref, far_ref, sems):
     copies = [
         pltpu.make_async_copy(src.at[:, z], dst.at[part], sems.at[z, part])
         for z, dst in ((1, up_ref), (0, down_ref))
@@ -32,6 +32,18 @@
         copy.start()
     for copy in copies:
         copy.wait()
+    low = lax.axis_index("gz") % 2 == 0
+
+    @pl.when(low)
+    def _():
+        near_ref[...] = up_ref[...]
+        far_ref[...] = down_ref[...]
+
+    @pl.when(jnp.logical_not(low))
+    def _():
+        near_ref[...] = down_ref[...]
+        far_ref[...] = up_ref[...]
+
     lanes = up_ref.shape[-1]
     lane = lane_index(up_ref.shape[2:])
     edge = jnp.zeros(up_ref.shape[2:], F32)
@@ -226,7 +238,7 @@
 
 
 def source_kernel(
-    down_ref, up_ref, local_ref, below_ref, above_ref, edge_ref, chip_ref, link_ref,
+    down_ref, up_ref, local_ref, inner_ref, outer_ref, edge_ref, chip_ref, link_ref,
     xi_ref, xo_ref, xp_ref, pieces_ref, part_ref, outer_part_ref, work, faces,
 ):
     _, _, nx, lanes = down_ref.shape
@@ -234,6 +246,7 @@
     scale = float(2 * nx * nx)
     lane = lane_index((SUBS, lanes))
     even = lax.axis_index("gy") % 2 == 0
+    low = lax.axis_index("gz") % 2 == 0
     for at in (pl.ds(i, SUBS) for i in range(0, nx, SUBS)):
         own, chip, link = edge_ref[at], chip_ref[at], link_ref[at]
         right, left = jnp.where(even, chip, link), jnp.where(even, link, chip)
@@ -247,9 +260,11 @@
     def load(c, k):
         f, z = divmod(c, 2)
         at = pl.ds(k, SUBS, stride=rows)
-        own, other = (up_ref, above_ref) if z else (down_ref, below_ref)
+        own = up_ref if z else down_ref
+        paired = low if z else jnp.logical_not(low)
+        other = [jnp.where(paired, inner_ref[part, f, at], outer_ref[part, f, at]) for part in range(2)]
         v, kap = own[0, f, at], own[1, f, at]
-        beyond = (0.5 * VERTICAL) * (kap + other[1, f, at]) * (other[0, f, at] - v)
+        beyond = (0.5 * VERTICAL) * (kap + other[1]) * (other[0] - v)
         upper = pltpu.roll(faces[0, at], lanes - 1 - c, 1)
         lower = pltpu.roll(faces[1, at], (lanes - c) % lanes, 1)
         side = jnp.where(lane == lanes - 1, upper, jnp.where(lane == 0, lower, 0.0))
@@ -313,13 +328,6 @@
     )(*args)
 
 
-def shift(values, axis, step):
-    peers = lax.axis_size(axis)
-    return lax.ppermute(
-        values, axis, [(i, i + step) for i in range(peers) if 0 <= i + step < peers]
-    )
-
-
 def exchange(pieces, axis):
     return lax.all_to_all(pieces, axis, 0, 0, axis_index_groups=[order(axis)])
 
@@ -334,12 +342,12 @@
     rows_x, rows_y = nx // SUBS, ny // SUBS
     gx, gy = lax.axis_size("gx"), lax.axis_size("gy")
     layer = struct(2, 2, nx, ny)
-    up, down, edge = call(
-        pack_kernel, [layer, layer, struct(nx, ny)], [pltpu.SemaphoreType.DMA((2, 2))],
+    up, down, edge, near, far = call(
+        pack_kernel, [layer, layer, struct(nx, ny), layer, layer], [pltpu.SemaphoreType.DMA((2, 2))],
         pltpu.with_memory_space_constraint(v, pltpu.HBM), pltpu.with_memory_space_constraint(kappa, pltpu.HBM), space=pltpu.HBM,
     )
-    below = shift(up, "gz", 1)
-    above = shift(down, "gz", -1)
+    inner = swap(near, "gz", 0)
+    outer = swap(far, "gz", 1)
     chip = swap(edge, "gy", 0)
     link = swap(edge, "gy", 1)
     work = pltpu.VMEM((3, 4 * SUBS, ny), F32)
@@ -358,7 +366,7 @@
         source_kernel,
         [struct(gx, 7, 4, ny), struct(4, rows_x - 1, SUBS, ny), struct(SUBS - 1, 4, ny)],
         [work, pltpu.VMEM((2, nx, ny), F32)],
-        down, up, local, below, above, edge, chip, link, xi, xo, xp,
+        down, up, local, inner, outer, edge, chip, link, xi, xo, xp,
     )
     pieces = exchange(pieces, "gx")
     pieces, y_part, y_outer = call(

time: 51.7 us -> 51.7 us (level)
  the two profiles are of different devices: /device:TPU:1 before, /device:TPU:9 now
where the time goes in v5:
time: 51.7 us; the launch traced here: 51.5 us
  blocking collectives  34.7 us (67%)
  starting transfers between devices  12.9 us (25%)
  Pallas kernels  3.41 us (7%)
    all_to_all x2, blocking collectives, exchange(): return lax.all_to_all(pieces, axis, 0, 0, axis_index_groups=[order(axis)])  34.7 us
    ppermute x4, starting transfers between devices, swap(): return lax.ppermute(values, axis, pairs + [(j, i) for i, j in pairs])  12.9 us
    pallas_call x5, Pallas kernels, call(): pl.pallas_call(kernel, out_shape=outs, in_specs=[pl.BlockSpec(memory_spac...  3.41 us
  transfers between devices with their start and end apart: 4, of which 1 were waited for; matrix products, arithmetic and copies ran while one was open for 0% of the time, Pallas kernels for 1%

profile of v5, /device:TPU:9, one launch (start us, length us, event | category | flops | bytes accessed | tf_op | source)
XLA Modules:
  0.0 51.5 jit_solution(1208289060201997665)
XLA Ops:
  0.0 0.0 copy-start
  0.0 1.2 %shard_map.37 = (f32[2,2,64,128]{3,2,1,0:T(8,128)S(1)}, f32[2,2,64,128]{3,2,1,0:T(8,128)S(1)}, f32[64,128]{1,0:T(8,128)S(1)}, f32[2,2,64,128]{3,2,1,0:T(8,128)S(1)}, f32[2,2,64,128]{3,2,1,0:T(8,128)S(1)}) custom-call(f32[2,2,64,128]{3,2,1,0:T(8,128)} %v_hbm.1, f32[2,2,64,128]{3,2,1,0:T(8,128)} %k_hbm.1), custom_call_target="tpu_custom_call" | custom-call | tf_op jit(solution)/shard_map/pallas_call | solution.py:321
  1.2 1.9 %collective-permute-start = (f32[2,2,64,128]{3,2,1,0:T(8,128)S(1)}, f32[2,2,64,128]{3,2,1,0:T(8,128)S(1)}, u32[]{:S(2)}, u32[]{:S(2)}) collective-permute-start(f32[2,2,64,128]{3,2,1,0:T(8,128)S(1)} %get-tuple-element.26), channel_id=1, source_target_pairs={{0,1},{2,3},{1,0},{3,2},{4,5},{6,7},{5,4},{7,6},{8,9},{10,11},{9,8... | collective-permute-start | bytes 393224 | tf_op jit(solution)/shard_map/ppermute | solution.py:337
  3.2 4.2 %collective-permute-start.1 = (f32[2,2,64,128]{3,2,1,0:T(8,128)S(1)}, f32[2,2,64,128]{3,2,1,0:T(8,128)S(1)}, u32[]{:S(2)}, u32[]{:S(2)}) collective-permute-start(f32[2,2,64,128]{3,2,1,0:T(8,128)S(1)} %get-tuple-element.27), channel_id=1, source_target_pairs={{1,2},{2,1},{5,6},{6,5},{9,10},{10,9},{13,14},{14,13},{17,18},{18,... | collective-permute-start | bytes 393224 | tf_op jit(solution)/shard_map/ppermute | solution.py:337
  7.4 4.2 %collective-permute-start.3 = (f32[64,128]{1,0:T(8,128)S(1)}, f32[64,128]{1,0:T(8,128)S(1)}, u32[]{:S(2)}, u32[]{:S(2)}) collective-permute-start(f32[64,128]{1,0:T(8,128)S(1)} %get-tuple-element.28.edge_ref), channel_id=1, source_target_pairs={{4,8},{12,16},{20,24},{8,4},{16,12},{24,20},{5,9},{13,17},{21,25},... | collective-permute-start | bytes 98312 | tf_op jit(solution)/shard_map/ppermute | solution.py:337
  11.6 2.5 %collective-permute-start.2 = (f32[64,128]{1,0:T(8,128)S(1)}, f32[64,128]{1,0:T(8,128)S(1)}, u32[]{:S(2)}, u32[]{:S(2)}) collective-permute-start(f32[64,128]{1,0:T(8,128)S(1)} %get-tuple-element.28.edge_ref), channel_id=1, source_target_pairs={{0,4},{8,12},{16,20},{24,28},{4,0},{12,8},{20,16},{28,24},{1,5},{9... | collective-permute-start | bytes 98312 | tf_op jit(solution)/shard_map/ppermute | solution.py:337
  14.2 0.0 copy-done
  14.2 0.4 shard_map.38
  14.6 0.0 collective-permute-done.3.link_ref
  14.6 0.4 collective-permute-done.2.chip_ref
  15.0 0.0 collective-permute-done.inner_ref
  15.0 0.0 collective-permute-done.1.outer_ref
  15.0 0.4 shard_map.39
  15.4 27.3 %all_to_all.10.pieces_ref = f32[16,7,4,128]{3,2,1,0:T(4,128)S(1)} all-to-all(f32[16,7,4,128]{3,2,1,0:T(4,128)S(1)} %get-tuple-element.32), channel_id=1, replica_groups={{320,32,0,64,96,480,448,416,128,384,160,352,192,288,224,256},{321,33,1,..., dimensions={0} | all-to-all | bytes 458752 | tf_op jit(solution)/shard_map/all_to_all | solution.py:332
  42.7 0.5 shard_map.40
  43.2 7.3 %all_to_all.11.pieces_ref = f32[8,7,2,128]{3,2,1,0:T(2,128)S(1)} all-to-all(f32[8,7,2,128]{3,2,1,0:T(2,128)S(1)} %get-tuple-element.38), channel_id=1, replica_groups={{20,16,0,4,8,12,28,24},{21,17,1,5,9,13,29,25},{22,18,2,6,10,14,30,26},{..., dimensions={0} | all-to-all | bytes 114688 | tf_op jit(solution)/shard_map/all_to_all | solution.py:332
  50.5 0.9 %shard_map.41 = f32[2,2,64,128]{3,2,1,0:T(8,128)} custom-call(f32[8,7,2,128]{3,2,1,0:T(2,128)S(1)} %all_to_all.11.pieces_ref, f32[2,2,64,128]{3,2,1,0:T(8,128)S(1)} %get-tuple-element.23.down_ref, f32[2,2,64,128]{3,2,1,0:T(8,128)S(1)} %get-tuple-element.24.up_ref, f32[3,2,15,8,128]{4,3,2,1,0:T(8,128)S(1)} %get-tuple-element.35.yi_ref, ...), custom_call_target="tpu_custom_call" | custom-call | tf_op jit(solution)/shard_map/pallas_call | solution.py:321
Async XLA Ops:
  0.0 14.2 %copy-start = (f32[2,2,64,128]{3,2,1,0:T(8,128)S(1)}, f32[2,2,64,128]{3,2,1,0:T(8,128)}, u32[]{:S(2)}) copy-start(f32[2,2,64,128]{3,2,1,0:T(8,128)} %s_ref.1) | copy-start | bytes 393220
  1.2 13.8 %collective-permute-start = (f32[2,2,64,128]{3,2,1,0:T(8,128)S(1)}, f32[2,2,64,128]{3,2,1,0:T(8,128)S(1)}, u32[]{:S(2)}, u32[]{:S(2)}) collective-permute-start(f32[2,2,64,128]{3,2,1,0:T(8,128)S(1)} %get-tuple-element.26), channel_id=1, source_target_pairs={{0,1},{2,3},{1,0},{3,2},{4,5},{6,7},{5,4},{7,6},{8,9},{10,11},{9,8... | collective-permute-start | bytes 393224 | tf_op jit(solution)/shard_map/ppermute | solution.py:337
  3.2 11.8 %collective-permute-start.1 = (f32[2,2,64,128]{3,2,1,0:T(8,128)S(1)}, f32[2,2,64,128]{3,2,1,0:T(8,128)S(1)}, u32[]{:S(2)}, u32[]{:S(2)}) collective-permute-start(f32[2,2,64,128]{3,2,1,0:T(8,128)S(1)} %get-tuple-element.27), channel_id=1, source_target_pairs={{1,2},{2,1},{5,6},{6,5},{9,10},{10,9},{13,14},{14,13},{17,18},{18,... | collective-permute-start | bytes 393224 | tf_op jit(solution)/shard_map/ppermute | solution.py:337
  7.4 7.2 %collective-permute-start.3 = (f32[64,128]{1,0:T(8,128)S(1)}, f32[64,128]{1,0:T(8,128)S(1)}, u32[]{:S(2)}, u32[]{:S(2)}) collective-permute-start(f32[64,128]{1,0:T(8,128)S(1)} %get-tuple-element.28.edge_ref), channel_id=1, source_target_pairs={{4,8},{12,16},{20,24},{8,4},{16,12},{24,20},{5,9},{13,17},{21,25},... | collective-permute-start | bytes 98312 | tf_op jit(solution)/shard_map/ppermute | solution.py:337
  11.6 3.4 %collective-permute-start.2 = (f32[64,128]{1,0:T(8,128)S(1)}, f32[64,128]{1,0:T(8,128)S(1)}, u32[]{:S(2)}, u32[]{:S(2)}) collective-permute-start(f32[64,128]{1,0:T(8,128)S(1)} %get-tuple-element.28.edge_ref), channel_id=1, source_target_pairs={{0,4},{8,12},{16,20},{24,28},{4,0},{12,8},{20,16},{28,24},{1,5},{9... | collective-permute-start | bytes 98312 | tf_op jit(solution)/shard_map/ppermute | solution.py:337

commit v6 on v5

--- a/solution.py
+++ b/solution.py
@@ -170,7 +170,7 @@
 
 
 def order(axis):
-    return {"gx": [10, 1, 0, 2, 3, 15, 14, 13, 4, 12, 5, 11, 6, 9, 7, 8], "gy": [5, 4, 0, 1, 2, 3, 7, 6]}[axis]
+    return {"gx": [9, 1, 0, 2, 3, 15, 14, 13, 4, 12, 5, 11, 6, 10, 7, 8], "gy": [5, 4, 0, 1, 7, 6, 2, 3]}[axis]
 
 
 def ends(pieces_ref, me, scale, order):

time: 51.7 us -> 52 us (level)
  the two profiles are of different devices: /device:TPU:9 before, /device:TPU:8 now
where the time goes in v6:
time: 52 us; the launch traced here: 51.7 us
  blocking collectives  34.1 us (66%)
  starting transfers between devices  12.2 us (23%)
  Pallas kernels  3.41 us (7%)
  waiting for transfers between devices  1.91 us (4%)
    all_to_all x2, blocking collectives, exchange(): return lax.all_to_all(pieces, axis, 0, 0, axis_index_groups=[order(axis)])  34.1 us
    ppermute x4, starting transfers between devices, swap(): return lax.ppermute(values, axis, pairs + [(j, i) for i, j in pairs])  12.2 us
    pallas_call x5, Pallas kernels, call(): pl.pallas_call(kernel, out_shape=outs, in_specs=[pl.BlockSpec(memory_spac...  3.41 us
    ppermute x4, waiting for transfers between devices, swap(): return lax.ppermute(values, axis, pairs + [(j, i) for i, j in pairs])  1.91 us
  transfers between devices with their start and end apart: 4, of which 2 were waited for; matrix products, arithmetic and copies ran while one was open for 0% of the time, Pallas kernels for 1%

profile of v6, /device:TPU:8, one launch (start us, length us, event | category | flops | bytes accessed | tf_op | source)
XLA Modules:
  0.0 51.7 jit_solution(2030896931849763163)
XLA Ops:
  0.0 0.0 copy-start
  0.0 1.2 %shard_map.37 = (f32[2,2,64,128]{3,2,1,0:T(8,128)S(1)}, f32[2,2,64,128]{3,2,1,0:T(8,128)S(1)}, f32[64,128]{1,0:T(8,128)S(1)}, f32[2,2,64,128]{3,2,1,0:T(8,128)S(1)}, f32[2,2,64,128]{3,2,1,0:T(8,128)S(1)}) custom-call(f32[2,2,64,128]{3,2,1,0:T(8,128)} %v_hbm.1, f32[2,2,64,128]{3,2,1,0:T(8,128)} %k_hbm.1), custom_call_target="tpu_custom_call" | custom-call | tf_op jit(solution)/shard_map/pallas_call | solution.py:321
  1.2 7.7 %collective-permute-start = (f32[2,2,64,128]{3,2,1,0:T(8,128)S(1)}, f32[2,2,64,128]{3,2,1,0:T(8,128)S(1)}, u32[]{:S(2)}, u32[]{:S(2)}) collective-permute-start(f32[2,2,64,128]{3,2,1,0:T(8,128)S(1)} %get-tuple-element.26), channel_id=1, source_target_pairs={{0,1},{2,3},{1,0},{3,2},{4,5},{6,7},{5,4},{7,6},{8,9},{10,11},{9,8... | collective-permute-start | bytes 393224 | tf_op jit(solution)/shard_map/ppermute | solution.py:337
  9.0 1.9 %collective-permute-start.1 = (f32[2,2,64,128]{3,2,1,0:T(8,128)S(1)}, f32[2,2,64,128]{3,2,1,0:T(8,128)S(1)}, u32[]{:S(2)}, u32[]{:S(2)}) collective-permute-start(f32[2,2,64,128]{3,2,1,0:T(8,128)S(1)} %get-tuple-element.27), channel_id=1, source_target_pairs={{1,2},{2,1},{5,6},{6,5},{9,10},{10,9},{13,14},{14,13},{17,18},{18,... | collective-permute-start | bytes 393224 | tf_op jit(solution)/shard_map/ppermute | solution.py:337
  10.9 0.7 %collective-permute-start.3 = (f32[64,128]{1,0:T(8,128)S(1)}, f32[64,128]{1,0:T(8,128)S(1)}, u32[]{:S(2)}, u32[]{:S(2)}) collective-permute-start(f32[64,128]{1,0:T(8,128)S(1)} %get-tuple-element.28.edge_ref), channel_id=1, source_target_pairs={{4,8},{12,16},{20,24},{8,4},{16,12},{24,20},{5,9},{13,17},{21,25},... | collective-permute-start | bytes 98312 | tf_op jit(solution)/shard_map/ppermute | solution.py:337
  11.6 1.9 %collective-permute-start.2 = (f32[64,128]{1,0:T(8,128)S(1)}, f32[64,128]{1,0:T(8,128)S(1)}, u32[]{:S(2)}, u32[]{:S(2)}) collective-permute-start(f32[64,128]{1,0:T(8,128)S(1)} %get-tuple-element.28.edge_ref), channel_id=1, source_target_pairs={{0,4},{8,12},{16,20},{24,28},{4,0},{12,8},{20,16},{28,24},{1,5},{9... | collective-permute-start | bytes 98312 | tf_op jit(solution)/shard_map/ppermute | solution.py:337
  13.5 0.0 copy-done
  13.5 0.4 shard_map.38
  13.9 0.0 collective-permute-done.3.link_ref
  13.9 0.7 %collective-permute-done.2.chip_ref = f32[64,128]{1,0:T(8,128)S(1)} collective-permute-done((f32[64,128]{1,0:T(8,128)S(1)}, f32[64,128]{1,0:T(8,128)S(1)}, u32[]{:S(2)}, u32[]{:S(2)}) %collective-permute-start.2) | collective-permute-done | bytes 32800 | tf_op jit(solution)/shard_map/ppermute | solution.py:337
  14.7 0.0 collective-permute-done.inner_ref
  14.7 1.2 %collective-permute-done.1.outer_ref = f32[2,2,64,128]{3,2,1,0:T(8,128)S(1)} collective-permute-done((f32[2,2,64,128]{3,2,1,0:T(8,128)S(1)}, f32[2,2,64,128]{3,2,1,0:T(8,128)S(1)}, u32[]{:S(2)}, u32[]{:S(2)}) %collective-permute-start.1) | collective-permute-done | bytes 131104 | tf_op jit(solution)/shard_map/ppermute | solution.py:337
  15.8 0.4 shard_map.39
  16.2 27.0 %all_to_all.10.pieces_ref = f32[16,7,4,128]{3,2,1,0:T(4,128)S(1)} all-to-all(f32[16,7,4,128]{3,2,1,0:T(4,128)S(1)} %get-tuple-element.32), channel_id=1, replica_groups={{288,32,0,64,96,480,448,416,128,384,160,352,192,320,224,256},{289,33,1,..., dimensions={0} | all-to-all | bytes 458752 | tf_op jit(solution)/shard_map/all_to_all | solution.py:332
  43.2 0.5 shard_map.40
  43.7 7.1 %all_to_all.11.pieces_ref = f32[8,7,2,128]{3,2,1,0:T(2,128)S(1)} all-to-all(f32[8,7,2,128]{3,2,1,0:T(2,128)S(1)} %get-tuple-element.38), channel_id=1, replica_groups={{20,16,0,4,28,24,8,12},{21,17,1,5,29,25,9,13},{22,18,2,6,30,26,10,14},{..., dimensions={0} | all-to-all | bytes 114688 | tf_op jit(solution)/shard_map/all_to_all | solution.py:332
  50.7 0.9 %shard_map.41 = f32[2,2,64,128]{3,2,1,0:T(8,128)} custom-call(f32[8,7,2,128]{3,2,1,0:T(2,128)S(1)} %all_to_all.11.pieces_ref, f32[2,2,64,128]{3,2,1,0:T(8,128)S(1)} %get-tuple-element.23.down_ref, f32[2,2,64,128]{3,2,1,0:T(8,128)S(1)} %get-tuple-element.24.up_ref, f32[3,2,15,8,128]{4,3,2,1,0:T(8,128)S(1)} %get-tuple-element.35.yi_ref, ...), custom_call_target="tpu_custom_call" | custom-call | tf_op jit(solution)/shard_map/pallas_call | solution.py:321
Async XLA Ops:
  0.0 13.5 %copy-start = (f32[2,2,64,128]{3,2,1,0:T(8,128)S(1)}, f32[2,2,64,128]{3,2,1,0:T(8,128)}, u32[]{:S(2)}) copy-start(f32[2,2,64,128]{3,2,1,0:T(8,128)} %s_ref.1) | copy-start | bytes 393220
  1.2 13.4 %collective-permute-start = (f32[2,2,64,128]{3,2,1,0:T(8,128)S(1)}, f32[2,2,64,128]{3,2,1,0:T(8,128)S(1)}, u32[]{:S(2)}, u32[]{:S(2)}) collective-permute-start(f32[2,2,64,128]{3,2,1,0:T(8,128)S(1)} %get-tuple-element.26), channel_id=1, source_target_pairs={{0,1},{2,3},{1,0},{3,2},{4,5},{6,7},{5,4},{7,6},{8,9},{10,11},{9,8... | collective-permute-start | bytes 393224 | tf_op jit(solution)/shard_map/ppermute | solution.py:337
  9.0 6.9 %collective-permute-start.1 = (f32[2,2,64,128]{3,2,1,0:T(8,128)S(1)}, f32[2,2,64,128]{3,2,1,0:T(8,128)S(1)}, u32[]{:S(2)}, u32[]{:S(2)}) collective-permute-start(f32[2,2,64,128]{3,2,1,0:T(8,128)S(1)} %get-tuple-element.27), channel_id=1, source_target_pairs={{1,2},{2,1},{5,6},{6,5},{9,10},{10,9},{13,14},{14,13},{17,18},{18,... | collective-permute-start | bytes 393224 | tf_op jit(solution)/shard_map/ppermute | solution.py:337
  10.9 3.0 %collective-permute-start.3 = (f32[64,128]{1,0:T(8,128)S(1)}, f32[64,128]{1,0:T(8,128)S(1)}, u32[]{:S(2)}, u32[]{:S(2)}) collective-permute-start(f32[64,128]{1,0:T(8,128)S(1)} %get-tuple-element.28.edge_ref), channel_id=1, source_target_pairs={{4,8},{12,16},{20,24},{8,4},{16,12},{24,20},{5,9},{13,17},{21,25},... | collective-permute-start | bytes 98312 | tf_op jit(solution)/shard_map/ppermute | solution.py:337
  11.6 3.1 %collective-permute-start.2 = (f32[64,128]{1,0:T(8,128)S(1)}, f32[64,128]{1,0:T(8,128)S(1)}, u32[]{:S(2)}, u32[]{:S(2)}) collective-permute-start(f32[64,128]{1,0:T(8,128)S(1)} %get-tuple-element.28.edge_ref), channel_id=1, source_target_pairs={{0,4},{8,12},{16,20},{24,28},{4,0},{12,8},{20,16},{28,24},{1,5},{9... | collective-permute-start | bytes 98312 | tf_op jit(solution)/shard_map/ppermute | solution.py:337
